TPU v7x, 32 devices: a whole 2x2x4 slice. The times are simulated.
32 devices in a mesh: slab: 4 (over y, x), energy: 8 (over z, core).
Axes of the slice: x: 2, y: 2, z: 4, core: 2. Of those that a mesh axis runs over, the one named last changes fastest.
Arguments:
- link_p: float32 [12, 2, 64, 64], P('slab'), may hold values from -1 to 2, as said below
- link_q: float32 [12, 2, 64, 64], P('slab'), may hold values from -1 to 2, as said below
- shift: float32 [64, 12, 64], P('energy', 'slab'), may hold values from 0.01 to 0.3
- lesser_gain: float32 [64, 12, 64], P('energy', 'slab'), may hold values from 0.1 to 2
- sources: float32 [12, 2, 64, 128], P('slab'), may hold values from -1.8 to 1.8
Outputs:
- polar: float32 [2, 64, 12, 64, 128], P(None, None, 'slab', 'energy')
Inputs may be any that keep to these rules, and one draw needn't show every extreme that they name: `link_p`: real and imaginary parts of complex link factors. `link_q`: real and imaginary parts of complex link factors.
All inputs are finite; a program needn't handle non-finite values.
Results may differ from a plain program's by a relative error of at most 0.0003.
Values sent between devices are 32-bit elements; how exact they have to be, the bound alone decides.
No kernel may reach another device: no remote copies, remote signals or barrier semaphores. Data moves between devices by JAX's collectives and lax.ppermute only.
A program may use at most 128 MiB of HBM per device.

v0:
```python
import math

import jax
import jax.numpy as jnp
from jax import lax
from jax.sharding import PartitionSpec as P

HIGHEST = lax.Precision.HIGHEST


def real_form(part):
    real = part[..., 0, :, :]
    imag = part[..., 1, :, :]
    upper_half = jnp.concatenate([real, -imag], axis=-1)
    lower_half = jnp.concatenate([imag, real], axis=-1)
    return jnp.concatenate([upper_half, lower_half], axis=-2)


def from_half(half):
    orbits = half.shape[-1]
    return real_form(jnp.stack([half[..., :orbits, :], half[..., orbits:, :]], axis=-3))


def right_transposed(left, right):
    return jnp.einsum("...ij,...kj->...ik", left, right, precision=HIGHEST)


def left_transposed(left, right):
    return jnp.einsum("...ji,...jk->...ik", left, right, precision=HIGHEST)


def product(left, right):
    return jnp.einsum("...ij,...jk->...ik", left, right, precision=HIGHEST)


def solve_with(factor, rhs):
    return jax.scipy.linalg.cho_solve((factor, True), rhs)


def forward_retarded(diag, upper, rhs):
    width = diag.shape[-1]
    opening = jnp.broadcast_to(jnp.swapaxes(upper[0], 0, 1), diag[1].shape)
    start = (diag[1], opening, rhs[1], diag[0], rhs[0])

    def sweep(carry, pieces):
        current, coupling, carried_rhs, corner, port_rhs = carry
        link_block, diag_after, rhs_after = pieces
        factor = jnp.linalg.cholesky(current)
        stacked = jnp.concatenate(
            [jnp.broadcast_to(link_block, current.shape), coupling, carried_rhs], axis=-1
        )
        solved = solve_with(factor, stacked)
        step_link = solved[..., :width]
        step_port = solved[..., width : 2 * width]
        step_rhs = solved[..., 2 * width :]
        corner = corner - left_transposed(coupling, step_port)
        port_rhs = port_rhs - left_transposed(coupling, step_rhs)
        current = diag_after - left_transposed(link_block, step_link)
        coupling = -left_transposed(link_block, step_port)
        carried_rhs = rhs_after - left_transposed(link_block, step_rhs)
        return (
            (current, coupling, carried_rhs, corner, port_rhs),
            (factor, step_link, step_port, step_rhs),
        )

    return lax.scan(sweep, start, (upper[1:], diag[2:], rhs[2:]))


def forward_lesser(factors, step_link, step_port, rhs):

    def sweep(carry, pieces):
        carried_rhs, port_rhs = carry
        factor, link_step, port_step, rhs_after = pieces
        step_rhs = solve_with(factor, carried_rhs)
        port_rhs = port_rhs - left_transposed(port_step, carried_rhs)
        carried_rhs = rhs_after - left_transposed(link_step, carried_rhs)
        return ((carried_rhs, port_rhs), step_rhs)

    final, steps = lax.scan(sweep, (rhs[1], rhs[0]), (factors, step_link, step_port, rhs[2:]))
    return (final[1], final[0], steps)


def back_substitute(step_link, step_port, step_rhs, first_port, last_port):

    def climb(carry, pieces):
        link_step, port_step, rhs_step = pieces
        value = rhs_step - product(link_step, carry) - product(port_step, first_port)
        return (value, value)

    unused, inner_rows = lax.scan(climb, last_port, (step_link, step_port, step_rhs), reverse=True)
    return jnp.concatenate([first_port[None], inner_rows, last_port[None]], axis=0)


def chain_factor(blocks, uppers):
    factors = []
    steps = []
    current = blocks[0]
    for position in range(len(blocks)):
        factor = jnp.linalg.cholesky(current)
        factors.append(factor)
        if position + 1 < len(blocks):
            step = solve_with(factor, uppers[position])
            steps.append(step)
            current = blocks[position + 1] - left_transposed(uppers[position], step)
    return (factors, steps)


def chain_solve(factors, steps, uppers, rhs_list):
    partial_rows = []
    carried = rhs_list[0]
    for position in range(len(factors)):
        solved = solve_with(factors[position], carried)
        partial_rows.append(solved)
        if position + 1 < len(factors):
            carried = rhs_list[position + 1] - left_transposed(uppers[position], solved)
    values = [partial_rows[-1]]
    for position in range(len(factors) - 2, -1, -1):
        values.insert(0, partial_rows[position] - product(steps[position], values[0]))
    return jnp.stack(values, axis=0)


def correlate(lesser_re, lesser_im, power):
    count = power.shape[1]
    length = 2 * count
    freqs = jnp.arange(length, dtype=jnp.int32)
    moments = jnp.arange(count, dtype=jnp.int32)
    phase = (freqs[:, None] * moments[None, :] % length).astype(jnp.float32) * (
        2.0 * math.pi / length
    )
    cos_table = jnp.cos(phase)
    sin_table = jnp.sin(phase)

    def transform(table, values):
        return jnp.einsum("kt,itor->kior", table, values, precision=HIGHEST)

    def inverse(table, values):
        return jnp.einsum("wk,kior->wior", table, values, precision=HIGHEST)

    spec_re = transform(cos_table, lesser_re) + transform(sin_table, lesser_im)
    spec_im = transform(cos_table, lesser_im) - transform(sin_table, lesser_re)
    power_cos = transform(cos_table, power)
    power_sin = transform(sin_table, power)
    mixed_re = spec_re * power_cos - spec_im * power_sin
    mixed_im = spec_re * power_sin + spec_im * power_cos
    scale = 1.0 / (length * count)
    back_cos = jnp.swapaxes(cos_table, 0, 1) * scale
    back_sin = jnp.swapaxes(sin_table, 0, 1) * scale
    corr_re = inverse(back_cos, mixed_re) - inverse(back_sin, mixed_im)
    corr_im = inverse(back_sin, mixed_re) + inverse(back_cos, mixed_im)
    return jnp.stack([corr_re, corr_im], axis=0)


def per_device(link_p, link_q, shift, lesser_gain, sources):
    slabs = link_p.shape[0]
    orbits = link_p.shape[2]
    width = 2 * orbits
    columns = sources.shape[-1]
    energies = shift.shape[0]
    owner = lax.axis_index("slab")
    devices = lax.axis_size("slab")
    rp = real_form(link_p)
    rq = real_form(link_q)
    pp = right_transposed(rp, rp)
    qq = right_transposed(rq, rq)
    cc = -right_transposed(rp, rq)
    lead = jnp.where(owner == 0, 1.0, 0.0).astype(jnp.float32)
    inner_sum = qq[:-1] + pp[1:]
    base = jnp.concatenate([(inner_sum[0] + lead * pp[0])[None], inner_sum[1:], qq[-1:]], axis=0)
    upper = cc[1:]
    eye = jnp.eye(width, dtype=jnp.float32)
    shift_slab = jnp.swapaxes(jnp.concatenate([shift, shift], axis=-1), 0, 1)
    diag = base[:, None] + eye * shift_slab[..., None, :]
    sources_flat = sources.reshape(slabs, width, columns)
    rhs = jnp.broadcast_to(sources_flat[:, None], (slabs, energies, width, columns))
    final, stored = forward_retarded(diag, upper, rhs)
    last_diag, coupling, last_rhs, corner, port_rhs = final
    factors, step_link, step_port, step_rhs = stored
    first_half = corner[..., :orbits]
    link_half = jnp.swapaxes(coupling, -1, -2)[..., :orbits]
    last_half = last_diag[..., :orbits]
    gathered = (
        lax.all_gather(first_half[None], "slab", axis=0, tiled=True),
        lax.all_gather(link_half[None], "slab", axis=0, tiled=True),
        lax.all_gather(last_half[None], "slab", axis=0, tiled=True),
        lax.all_gather(port_rhs[None], "slab", axis=0, tiled=True),
        lax.all_gather(last_rhs[None], "slab", axis=0, tiled=True),
        lax.all_gather(cc[0][..., :orbits][None], "slab", axis=0, tiled=True),
        lax.all_gather(pp[0][..., :orbits][None], "slab", axis=0, tiled=True),
    )
    heads, links, tails, head_rhs, tail_rhs, left_links, left_terms = gathered
    blocks = []
    uppers = []
    rhs_list = []
    for member in range(devices):
        blocks.append(from_half(heads[member]))
        tail_block = from_half(tails[member])
        rhs_list.append(head_rhs[member])
        rhs_list.append(tail_rhs[member])
        uppers.append(from_half(links[member]))
        if member + 1 < devices:
            tail_block = tail_block + from_half(left_terms[member + 1])
            uppers.append(jnp.broadcast_to(from_half(left_links[member + 1]), tail_block.shape))
        blocks.append(tail_block)
    chain_factors, chain_steps = chain_factor(blocks, uppers)
    ports = chain_solve(chain_factors, chain_steps, uppers, rhs_list)
    first_port = lax.dynamic_index_in_dim(ports, 2 * owner, 0, keepdims=False)
    last_port = lax.dynamic_index_in_dim(ports, 2 * owner + 1, 0, keepdims=False)
    retarded = back_substitute(step_link, step_port, step_rhs, first_port, last_port)
    gain_slab = jnp.swapaxes(jnp.concatenate([lesser_gain, lesser_gain], axis=-1), 0, 1)
    lesser_rhs = gain_slab[..., None] * retarded
    head_lesser, tail_lesser, lesser_steps = forward_lesser(
        factors, step_link, step_port, lesser_rhs
    )
    lesser_heads, lesser_tails = (
        lax.all_gather(head_lesser[None], "slab", axis=0, tiled=True),
        lax.all_gather(tail_lesser[None], "slab", axis=0, tiled=True),
    )
    lesser_list = []
    for member in range(devices):
        lesser_list.append(lesser_heads[member])
        lesser_list.append(lesser_tails[member])
    lesser_ports = chain_solve(chain_factors, chain_steps, uppers, lesser_list)
    first_lesser = lax.dynamic_index_in_dim(lesser_ports, 2 * owner, 0, keepdims=False)
    last_lesser = lax.dynamic_index_in_dim(lesser_ports, 2 * owner + 1, 0, keepdims=False)
    lesser = back_substitute(step_link, step_port, lesser_steps, first_lesser, last_lesser)
    ret_real = retarded[:, :, :orbits]
    ret_imag = retarded[:, :, orbits:]
    les_real = lesser[:, :, :orbits]
    les_imag = lesser[:, :, orbits:]
    elem_re = ret_real * les_real + ret_imag * les_imag
    elem_im = ret_real * les_imag - ret_imag * les_real
    elem_power = ret_real * ret_real + ret_imag * ret_imag
    return correlate(
        lax.all_to_all(elem_re, "energy", split_axis=2, concat_axis=1, tiled=True),
        lax.all_to_all(elem_im, "energy", split_axis=2, concat_axis=1, tiled=True),
        lax.all_to_all(elem_power, "energy", split_axis=2, concat_axis=1, tiled=True),
    )


def solution(mesh):
    placed = (
        P("slab", None, None, None),
        P("slab", None, None, None),
        P("energy", "slab", None),
        P("energy", "slab", None),
        P("slab", None, None, None),
    )
    return jax.shard_map(
        per_device,
        mesh=mesh,
        in_specs=placed,
        out_specs=P(None, None, "slab", "energy", None),
        check_vma=False,
    )
```

profile of v0, /device:TPU:0, one launch (start us, length us, event | category | flops | bytes accessed | tf_op | source)
XLA Modules:
  0.0 1964.4 jit_solution(12162616575540330299)
XLA Ops:
  12.5 94.0 %custom-call.48 = f32[8,128,128]{2,1,0:T(8,128)S(1)} custom-call(f32[8,128,128]{2,1,0:T(8,128)S(1)} %fusion.35), custom_call_target="Cholesky" | custom-call | tf_op jit(solution)/shard_map/while/body/eval_jaxpr/jit(cholesky)/cholesky | solution.py:48
  106.8 78.6 %custom-call.16 = f32[8,1,128,128]{2,3,1,0:T(8,128)S(1)} custom-call(f32[8,1,128,128]{3,2,1,0:T(8,128)S(1)} %fusion.145), custom_call_target="InvertDiagBlocksLowerTriangular" | custom-call | tf_op jit(solution)/shard_map/while/body/eval_jaxpr/jit(_cho_solve)/vmap()/triangular_solve | solution.py:37
  199.5 11.1 all-gather.4
  210.9 10.5 all-gather.6
  225.8 3.4 slice_negate_fusion.2
  229.8 93.8 %custom-call.49 = f32[8,128,128]{2,1,0:T(8,128)S(1)} custom-call(f32[8,128,128]{2,1,0:T(8,128)S(1)} %fusion.137), custom_call_target="Cholesky" | custom-call | tf_op jit(solution)/shard_map/jit(cholesky)/cholesky | solution.py:99
  323.9 78.6 %custom-call.50 = f32[8,1,128,128]{2,3,1,0:T(8,128)S(1)} custom-call(f32[8,1,128,128]{3,2,1,0:T(8,128)S(1)} %select_bitcast_fusion.7), custom_call_target="InvertDiagBlocksLowerTriangular" | custom-call | tf_op jit(solution)/shard_map/jit(_cho_solve)/vmap()/triangular_solve | solution.py:37
  402.5 3.0 fusion.272
  407.7 3.4 slice_negate_fusion.1
  415.6 94.0 %custom-call.52 = f32[8,128,128]{2,1,0:T(8,128)S(1)} custom-call(f32[8,128,128]{2,1,0:T(8,128)S(1)} %fusion.126), custom_call_target="Cholesky" | custom-call | tf_op jit(solution)/shard_map/jit(cholesky)/cholesky | solution.py:99
  509.9 78.6 %custom-call.53 = f32[8,1,128,128]{2,3,1,0:T(8,128)S(1)} custom-call(f32[8,1,128,128]{3,2,1,0:T(8,128)S(1)} %select_bitcast_fusion.6), custom_call_target="InvertDiagBlocksLowerTriangular" | custom-call | tf_op jit(solution)/shard_map/jit(_cho_solve)/vmap()/triangular_solve | solution.py:37
  595.1 94.8 %custom-call.55 = f32[8,128,128]{2,1,0:T(8,128)S(1)} custom-call(f32[8,128,128]{2,1,0:T(8,128)} %fusion.113), custom_call_target="Cholesky" | custom-call | tf_op jit(solution)/shard_map/jit(cholesky)/cholesky | solution.py:99
  691.0 79.4 %custom-call.56 = f32[8,1,128,128]{2,3,1,0:T(8,128)S(1)} custom-call(f32[8,1,128,128]{3,2,1,0:T(8,128)} %select_bitcast_fusion.5), custom_call_target="InvertDiagBlocksLowerTriangular" | custom-call | tf_op jit(solution)/shard_map/jit(_cho_solve)/vmap()/triangular_solve | solution.py:37
  784.1 95.6 %custom-call.58 = f32[8,128,128]{2,1,0:T(8,128)} custom-call(f32[8,128,128]{2,1,0:T(8,128)} %fusion.100), custom_call_target="Cholesky" | custom-call | tf_op jit(solution)/shard_map/jit(cholesky)/cholesky | solution.py:99
  882.9 80.0 %custom-call.59 = f32[8,1,128,128]{2,3,1,0:T(8,128)} custom-call(f32[8,1,128,128]{3,2,1,0:T(8,128)} %select_bitcast_fusion.4), custom_call_target="InvertDiagBlocksLowerTriangular" | custom-call | tf_op jit(solution)/shard_map/jit(_cho_solve)/vmap()/triangular_solve | solution.py:37
  973.5 95.4 %custom-call.61 = f32[8,128,128]{2,1,0:T(8,128)} custom-call(f32[8,128,128]{2,1,0:T(8,128)} %fusion.87), custom_call_target="Cholesky" | custom-call | tf_op jit(solution)/shard_map/jit(cholesky)/cholesky | solution.py:99
  1072.1 80.0 %custom-call.62 = f32[8,1,128,128]{2,3,1,0:T(8,128)} custom-call(f32[8,1,128,128]{3,2,1,0:T(8,128)} %select_bitcast_fusion.3), custom_call_target="InvertDiagBlocksLowerTriangular" | custom-call | tf_op jit(solution)/shard_map/jit(_cho_solve)/vmap()/triangular_solve | solution.py:37
  1166.0 95.4 %custom-call.64 = f32[8,128,128]{2,1,0:T(8,128)} custom-call(f32[8,128,128]{2,1,0:T(8,128)} %fusion.74), custom_call_target="Cholesky" | custom-call | tf_op jit(solution)/shard_map/jit(cholesky)/cholesky | solution.py:99
  1264.6 80.1 %custom-call.65 = f32[8,1,128,128]{2,3,1,0:T(8,128)} custom-call(f32[8,1,128,128]{3,2,1,0:T(8,128)} %select_bitcast_fusion.2), custom_call_target="InvertDiagBlocksLowerTriangular" | custom-call | tf_op jit(solution)/shard_map/jit(_cho_solve)/vmap()/triangular_solve | solution.py:37
  1355.2 95.7 %custom-call.67 = f32[8,128,128]{2,1,0:T(8,128)} custom-call(f32[8,128,128]{2,1,0:T(8,128)} %fusion.61), custom_call_target="Cholesky" | custom-call | tf_op jit(solution)/shard_map/jit(cholesky)/cholesky | solution.py:99
  1454.1 80.0 %custom-call.68 = f32[8,1,128,128]{2,3,1,0:T(8,128)} custom-call(f32[8,1,128,128]{3,2,1,0:T(8,128)} %select_bitcast_fusion.1), custom_call_target="InvertDiagBlocksLowerTriangular" | custom-call | tf_op jit(solution)/shard_map/jit(_cho_solve)/vmap()/triangular_solve | solution.py:37
  1547.9 95.2 %custom-call.70 = f32[8,128,128]{2,1,0:T(8,128)} custom-call(f32[8,128,128]{2,1,0:T(8,128)} %fusion.48), custom_call_target="Cholesky" | custom-call | tf_op jit(solution)/shard_map/jit(cholesky)/cholesky | solution.py:99
  1646.3 80.2 %custom-call.71 = f32[8,1,128,128]{2,3,1,0:T(8,128)} custom-call(f32[8,1,128,128]{3,2,1,0:T(8,128)} %select_bitcast_fusion), custom_call_target="InvertDiagBlocksLowerTriangular" | custom-call | tf_op jit(solution)/shard_map/jit(_cho_solve)/vmap()/triangular_solve | solution.py:37
  1763.9 3.0 convolution_subtract_fusion.18
  1770.8 29.1 %all-gather.27.cloned.1.call-done = f32[32,128,128]{2,1,0:T(8,128)} async-done(((f32[8,128,128]{2,1,0:T(8,128)}), f32[32,128,128]{2,1,0:T(8,128)}) %all-gather.27.cloned.1.call-update) | async-done | bytes 2097168 | tf_op jit(solution)/shard_map/all_gather | solution.py:215
  1803.4 33.7 %all-gather.29.cloned.1.call-done = f32[32,128,128]{2,1,0:T(8,128)} async-done(((f32[8,128,128]{2,1,0:T(8,128)}), f32[32,128,128]{2,1,0:T(8,128)}) %all-gather.29.cloned.1.call-update) | async-done | bytes 2097168 | tf_op jit(solution)/shard_map/all_gather | solution.py:216
  1870.9 4.6 all-to-all-start
  1876.8 19.6 all-to-all-done
  1896.4 3.5 all-to-all-start.2
  1901.3 19.5 all-to-all-done.2
  1920.9 3.7 all-to-all-start.1
  1932.8 12.6 all-to-all-done.1
  (476 shorter events, 218.2 us)
Async XLA Ops:
  6.5 219.2 %all-gather.17.cloned.1.call-start = ((), (), s32[]{:S(2)}) async-start(), calls=%async_computation.3 | async-start | bytes 1310720 | tf_op jit(solution)/shard_map/all_gather | solution.py:182
  12.4 173.8 %copy-start.106 = (f32[3,2,64,128]{3,2,1,0:T(8,128)S(1)}, f32[3,2,64,128]{3,2,1,0:T(8,128)}, u32[]{:S(2)}) copy-start(f32[3,2,64,128]{3,2,1,0:T(8,128)} %param.12) | copy-start | bytes 589828
  191.8 210.7 %all-gather.21.cloned.1.call-start = ((), (), s32[]{:S(2)}) async-start(), calls=%async_computation.5 | async-start | bytes 1310720 | tf_op jit(solution)/shard_map/all_gather | solution.py:183
  193.2 214.5 %all-gather.23.cloned.1.call-start = ((), (), s32[]{:S(2)}) async-start(), calls=%async_computation.6 | async-start | bytes 1310720 | tf_op jit(solution)/shard_map/all_gather | solution.py:184
  195.4 1531.0 %all-gather.19.cloned.1.call-start = ((), (), s32[]{:S(2)}) async-start(), calls=%async_computation.4 | async-start | bytes 2621440 | tf_op jit(solution)/shard_map/all_gather | solution.py:185
  197.3 1532.7 %all-gather.25.cloned.1.call-start = ((), (), s32[]{:S(2)}) async-start(), calls=%async_computation.7 | async-start | bytes 2621440 | tf_op jit(solution)/shard_map/all_gather | solution.py:186
  197.5 13.4 copy-start.107
  199.5 22.6 %copy-start.109 = (f32[8,3,64]{2,0,1:T(8,128)S(1)}, f32[8,3,64]{2,0,1:T(8,128)}, u32[]{:S(2)}) copy-start(f32[8,3,64]{2,0,1:T(8,128)} %param.11) | copy-start | bytes 18436
  199.5 1600.4 %all-gather.27.cloned.1.call-start = ((), (), s32[]{:S(2)}) async-start(), calls=%async_computation.8 | async-start | bytes 2621440 | tf_op jit(solution)/shard_map/all_gather | solution.py:215
  405.7 5.5 copy-start.10
  405.7 5.5 copy-start.48
  405.8 5.3 copy-start.49
  414.5 174.0 %copy-start.78 = (f32[128,128]{0,1:T(8,128)S(1)}, f32[128,128]{0,1:T(8,128)}, u32[]{:S(2)}) copy-start(f32[128,128]{0,1:T(8,128)} %maximum_maximum_fusion.12) | copy-start | bytes 196612
  771.5 5.6 copy-start.11
  782.1 180.9 %copy-start.75 = (f32[128,128]{0,1:T(8,128)S(1)}, f32[128,128]{0,1:T(8,128)}, u32[]{:S(2)}) copy-start(f32[128,128]{0,1:T(8,128)} %maximum_maximum_fusion.14) | copy-start | bytes 196612
  963.0 4.6 copy-start.89
  963.0 4.6 copy-start.90
  963.0 4.6 copy-start.91
  1153.2 5.8 copy-start.14
  1155.8 4.1 copy-start.56
  1155.8 4.1 copy-start.59
  1155.8 4.1 copy-start.92
  1155.8 4.1 copy-start.93
  1155.8 4.1 copy-start.94
  1264.6 84.7 %copy-start.86 = (f32[8,64,64]{1,2,0:T(8,128)S(1)}, f32[8,64,64]{1,2,0:T(8,128)}, u32[]{:S(2)}) copy-start(f32[8,64,64]{1,2,0:T(8,128)} %get-tuple-element.146) | copy-start | bytes 393220
  1344.7 4.6 copy-start.87
  1344.7 4.6 copy-start.88
  1763.9 73.2 %all-gather.29.cloned.1.call-start = ((), (), s32[]{:S(2)}) async-start(), calls=%async_computation.9 | async-start | bytes 2621440 | tf_op jit(solution)/shard_map/all_gather | solution.py:216
  1869.5 6.0 copy-start.69
  1870.9 25.6 %all-to-all-start = ((f32[3,8,64,128]{3,1,0,2:T(8,128)}), f32[3,8,64,128]{3,1,0,2:T(8,128)S(1)}, u32[]{:S(2)}, u32[]{:S(2)}) async-start(f32[3,8,64,128]{3,1,0,2:T(8,128)} %copy.243), calls=%async_computation | async-start | bytes 1572864 | tf_op jit(solution)/shard_map/all_to_all | solution.py:234
  1896.4 24.5 %all-to-all-start.2 = ((f32[3,8,64,128]{3,1,0,2:T(8,128)}), f32[3,8,64,128]{3,1,0,2:T(8,128)S(1)}, u32[]{:S(2)}, u32[]{:S(2)}) async-start(f32[3,8,64,128]{3,1,0,2:T(8,128)} %copy.247), calls=%async_computation.2 | async-start | bytes 1572864 | tf_op jit(solution)/shard_map/all_to_all | solution.py:236
  1920.9 24.5 %all-to-all-start.1 = ((f32[3,8,64,128]{3,1,0,2:T(8,128)}), f32[3,8,64,128]{3,1,0,2:T(8,128)S(1)}, u32[]{:S(2)}, u32[]{:S(2)}) async-start(f32[3,8,64,128]{3,1,0,2:T(8,128)} %copy.245), calls=%async_computation.1 | async-start | bytes 1572864 | tf_op jit(solution)/shard_map/all_to_all | solution.py:235
  (88 other events, 174.5 us)
Sparse Core Ops, SparseCore 0:
  191.9 30.8 all-gather.16
  224.6 26.9 all-gather.20
  253.5 26.8 all-gather.22
  282.0 35.6 all-gather.18
  319.4 36.2 all-gather.24
  1764.0 35.8 all-gather.26
  1801.7 35.2 all-gather.28
where the time goes:
time: 1970 us; the launch traced here: 1960 us
  other arithmetic  1620 us (82%)
  matrix products  129 us (7%)
  waiting for transfers between devices  115 us (6%)
  local copies, waits for them, and re-layouts  49.9 us (3%)
  blocking collectives  21.6 us (1%)
    another operation x25, other arithmetic, chain_factor(): factor = jnp.linalg.cholesky(current)  766 us
    another operation x19, other arithmetic, solve_with(): return jax.scipy.linalg.cho_solve((factor, True), rhs)  727 us
    another operation x3, other arithmetic, sweep(): factor = jnp.linalg.cholesky(current)  94.1 us
    another operation x50, matrix products, solve_with(): return jax.scipy.linalg.cho_solve((factor, True), rhs)  57.9 us
    dot_general x28, matrix products, left_transposed(): return jnp.einsum('...ji,...jk->...ik', left, right, precision=HIGHEST)  39.4 us
  transfers between devices with their start and end apart: 10, of which 5 were waited for; matrix products, arithmetic and copies ran while one was open for 78% of the time, Pallas kernels for 0%

commit v1 on v0

v1 whole, which is shorter than its diff:
```python
import functools

import jax
import jax.numpy as jnp
from jax import lax
from jax.experimental import pallas as pl
from jax.experimental.pallas import tpu as pltpu
from jax.sharding import PartitionSpec as P

HIGHEST = lax.Precision.HIGHEST
F32 = jnp.float32
VMEM_LIMIT = 56 * 1024 * 1024
PANEL = 8


def elimination_levels(count):
    levels = []
    chain = list(range(count))
    while len(chain) > 1:
        level = []
        for place in range(0, len(chain), 2):
            left = chain[place - 1] if place > 0 else None
            right = chain[place + 1] if place + 1 < len(chain) else None
            level.append((chain[place], left, right))
        levels.append(level)
        chain = chain[1::2]
    return levels, chain[0]


def mm(a, b):
    return lax.dot_general(a, b, (((1,), (0,)), ((), ())), precision=HIGHEST, preferred_element_type=F32)


def mm_nt(a, b):
    return lax.dot_general(a, b, (((1,), (1,)), ((), ())), precision=HIGHEST, preferred_element_type=F32)


def half_roll(x):
    return pltpu.roll(x, x.shape[1] // 2, 1)


def invert_batch(mat_ref, members, orbits):
    width = 2 * orbits
    blocks = orbits // PANEL
    lane = lax.broadcasted_iota(jnp.int32, (PANEL, width), 1)
    sub = lax.broadcasted_iota(jnp.int32, (PANEL, width), 0)
    pivots = (lane < PANEL) | ((lane >= orbits) & (lane < orbits + PANEL))

    def panel(p, unused):
        rows = pl.ds(pl.multiple_of(p * PANEL, PANEL), PANEL)
        original = lax.rem(lane + p * PANEL, width)
        sign = jnp.where(original < orbits, -1.0, 1.0).astype(F32)
        tops = []
        for m in members:
            tops.append(mat_ref[m, rows, :])
        for k in range(PANEL):
            here = sub == k
            at_pivot = (lane == k) | (lane == orbits + k)
            unit = jnp.where(here & (lane == k), 1.0, 0.0).astype(F32)
            for n in range(len(tops)):
                r = tops[n]
                cr = jnp.broadcast_to(r[:, k : k + 1], r.shape)
                ci = jnp.broadcast_to(r[:, orbits + k : orbits + k + 1], r.shape)
                inv = 1.0 / cr[k : k + 1, :]
                r0 = jnp.where(at_pivot, unit, r)
                row = r0[k : k + 1, :] * inv
                hat = half_roll(r0)[k : k + 1, :] * (sign[k : k + 1, :] * inv)
                tops[n] = jnp.where(here, row, r0 - cr * row - ci * hat)
        for n, m in enumerate(members):
            r = tops[n]
            hat = half_roll(r) * sign
            for i in range(blocks):
                block = mat_ref[m, PANEL * i : PANEL * (i + 1), :]
                out = jnp.where(pivots, 0.0, block)
                for j in range(PANEL):
                    out = out - jnp.broadcast_to(block[:, j : j + 1], out.shape) * r[j : j + 1, :]
                    out = out - jnp.broadcast_to(block[:, orbits + j : orbits + j + 1], out.shape) * hat[j : j + 1, :]
                mat_ref[m, PANEL * i : PANEL * (i + 1), :] = pltpu.roll(out, width - PANEL, 1)
            mat_ref[m, rows, :] = pltpu.roll(r, width - PANEL, 1)
        return 0

    lax.fori_loop(0, blocks, panel, 0)


def solve_kernel(plan, first_ref, data_ref, out_ref, mat, rhs, inv, w1, w2, sol, up1, dn1, up2, dn2):
    (slabs, mine, orbits, groups, energy_groups, per, orb_per) = plan
    width = 2 * orbits
    levels, root = elimination_levels(slabs)
    lane = lax.broadcasted_iota(jnp.int32, (orbits, width), 1)
    sub = lax.broadcasted_iota(jnp.int32, (orbits, width), 0)
    low = lane < orbits
    diag_lane = lane == sub
    gain_lane = lane == sub + orbits
    first = first_ref[0]

    def real_rows(z):
        return jnp.concatenate([jnp.where(low, z, -z), half_roll(z)], axis=0)

    def trans_rows(z):
        return jnp.concatenate([z, jnp.where(low, -half_roll(z), half_roll(z))], axis=0)

    def real_left(t):
        top, bottom = t[:orbits], t[orbits:]
        return jnp.concatenate(
            [jnp.where(low, top, -half_roll(bottom)), jnp.where(low, bottom, half_roll(top))], axis=0
        )

    def real_right(t):
        top, bottom = t[:orbits], t[orbits:]
        return jnp.concatenate(
            [jnp.where(low, half_roll(top), -bottom), jnp.where(low, half_roll(bottom), top)], axis=0
        )

    def packed_left(t):
        return jnp.where(low, t[:orbits], half_roll(t[orbits:]))

    def packed_right(t):
        return jnp.where(low, half_roll(t[:orbits]), t[orbits:])

    def factor_p(s):
        return data_ref[s, 0:orbits, :]

    def factor_q(s):
        return data_ref[s, orbits : 2 * orbits, :]

    def settings(s, e):
        return data_ref[s, pl.ds(4 * orbits + first + e, 1), :]

    for s in range(slabs):
        zq = factor_q(s)
        base = mm_nt(zq, trans_rows(zq))
        if s + 1 < slabs:
            zp = factor_p(s + 1)
            base = base + mm_nt(zp, trans_rows(zp))
            rp = real_rows(zp)
            rq = real_rows(factor_q(s + 1))
            up1[s] = -mm_nt(rp, rq)
            dn1[s] = -mm_nt(rq, rp)
        if s == 0:
            zp = factor_p(0)
            base = base + mm_nt(zp, trans_rows(zp))
        for e in range(mine):
            mat[s * mine + e] = base + jnp.where(diag_lane, settings(s, e), 0.0)
            rhs[s * mine + e] = data_ref[s, 2 * orbits : 4 * orbits, :]

    links = {}
    for s in range(slabs - 1):
        for e in range(mine):
            links[(0, s, s + 1, e)] = (up1, dn1, s)
    spare = 0
    for depth, level in enumerate(levels):
        for node, left, right in level:
            if left is not None and right is not None:
                for e in range(mine):
                    links[(depth + 1, left, right, e)] = (up2, dn2, spare)
                    spare += 1

    def links_of(depth, node, left, right, e):
        from_left = from_right = None
        if left is not None:
            refs = links[(depth, left, node, e)]
            from_left = refs[0][refs[2]]
        if right is not None:
            refs = links[(depth, node, right, e)]
            from_right = refs[1][refs[2]]
        return from_left, from_right

    def couplings(depth, node, left, right, e):
        pieces = [None, None]
        if left is not None:
            refs = links[(depth, left, node, e)]
            pieces[0] = refs[1][refs[2]]
        if right is not None:
            refs = links[(depth, node, right, e)]
            pieces[1] = half_roll(refs[0][refs[2]])
        low_all = lax.broadcasted_iota(jnp.int32, (width, width), 1) < orbits
        if pieces[0] is None:
            return jnp.where(low_all, 0.0, pieces[1])
        if pieces[1] is None:
            return jnp.where(low_all, pieces[0], 0.0)
        return jnp.where(low_all, pieces[0], pieces[1])

    def expand_inverse(m):
        inv[m] = real_rows(half_roll(mat[m]))

    for depth, level in enumerate(levels):
        invert_batch(mat, [node * mine + e for node, _, _ in level for e in range(mine)], orbits)
        for node, left, right in level:
            for e in range(mine):
                m = node * mine + e
                expand_inverse(m)
                stacked = jnp.concatenate([couplings(depth, node, left, right, e), rhs[m]], axis=1)
                step = mm(inv[m], stacked)
                links_step, rhs_step = step[:, :width], step[:, width:]
                from_left, from_right = links_of(depth, node, left, right, e)
                sol[m] = rhs_step
                if left is not None:
                    w1[m] = real_left(links_step)
                    change = mm(from_left, step)
                    ml = left * mine + e
                    mat[ml] = mat[ml] - packed_left(change[:, :width])
                    rhs[ml] = rhs[ml] - change[:, width:]
                    if right is not None:
                        refs = links[(depth + 1, left, right, e)]
                        refs[0][refs[2]] = -real_right(change[:, :width])
                if right is not None:
                    w2[m] = real_right(links_step)
                    change = mm(from_right, step)
                    mr = right * mine + e
                    mat[mr] = mat[mr] - packed_right(change[:, :width])
                    rhs[mr] = rhs[mr] - change[:, width:]
                    if left is not None:
                        refs = links[(depth + 1, left, right, e)]
                        refs[1][refs[2]] = -real_left(change[:, :width])
    invert_batch(mat, [root * mine + e for e in range(mine)], orbits)
    for e in range(mine):
        m = root * mine + e
        expand_inverse(m)
        sol[m] = mm(inv[m], rhs[m])

    def climb():
        for level in reversed(levels):
            for node, left, right in level:
                for e in range(mine):
                    m = node * mine + e
                    if left is not None and right is not None:
                        both = jnp.concatenate([w1[m], w2[m]], axis=1)
                        sides = jnp.concatenate([sol[left * mine + e], sol[right * mine + e]], axis=0)
                        sol[m] = sol[m] - mm(both, sides)
                    elif left is not None:
                        sol[m] = sol[m] - mm(w1[m], sol[left * mine + e])
                    elif right is not None:
                        sol[m] = sol[m] - mm(w2[m], sol[right * mine + e])

    climb()

    def deliver(what, s, e, value):
        for j in range(energy_groups):
            out_ref[s // per, j, what, e, s % per, :, :] = value[j * orb_per : (j + 1) * orb_per, :]

    for s in range(slabs):
        for e in range(mine):
            m = s * mine + e
            gain = jnp.sum(jnp.where(gain_lane, settings(s, e), 0.0), axis=1, keepdims=True)
            x = sol[m]
            rhs[m] = x * jnp.concatenate([gain, gain], axis=0)
            inverse_left = x
            keep = inverse_left
            xr, xi = keep[:orbits], keep[orbits:]
            deliver(2, s, e, xr * xr + xi * xi)
    ret = {}
    for s in range(slabs):
        for e in range(mine):
            ret[(s, e)] = s * mine + e
    return (levels, root, ret, links_of, climb, deliver)


def kernel_body(plan, first_ref, data_ref, out_ref, mat, rhs, inv, w1, w2, sol, up1, dn1, up2, dn2, kept):
    (slabs, mine, orbits, groups, energy_groups, per, orb_per) = plan
    levels, root, _, links_of, climb, deliver = solve_kernel(
        plan, first_ref, data_ref, out_ref, mat, rhs, inv, w1, w2, sol, up1, dn1, up2, dn2
    )
    for m in range(slabs * mine):
        kept[m] = sol[m]
    for depth, level in enumerate(levels):
        for node, left, right in level:
            for e in range(mine):
                m = node * mine + e
                step = mm(inv[m], rhs[m])
                sol[m] = step
                from_left, from_right = links_of(depth, node, left, right, e)
                if left is not None:
                    ml = left * mine + e
                    rhs[ml] = rhs[ml] - mm(from_left, step)
                if right is not None:
                    mr = right * mine + e
                    rhs[mr] = rhs[mr] - mm(from_right, step)
    for e in range(mine):
        m = root * mine + e
        sol[m] = mm(inv[m], rhs[m])
    climb()
    for s in range(slabs):
        for e in range(mine):
            m = s * mine + e
            x, y = kept[m], sol[m]
            xr, xi, yr, yi = x[:orbits], x[orbits:], y[:orbits], y[orbits:]
            deliver(0, s, e, xr * yr + xi * yi)
            deliver(1, s, e, xr * yi - xi * yr)


def solve_slabs(first, data, plan):
    (slabs, mine, orbits, groups, energy_groups, per, orb_per) = plan
    width = 2 * orbits
    columns = data.shape[-1]
    nodes = slabs * mine
    levels, _ = elimination_levels(slabs)
    fills = mine * sum(1 for level in levels for _, a, b in level if a is not None and b is not None)
    square = (width, width)
    return pl.pallas_call(
        functools.partial(kernel_body, plan),
        out_shape=jax.ShapeDtypeStruct((groups, energy_groups, 3, mine, per, orb_per, columns), F32),
        in_specs=[
            pl.BlockSpec(memory_space=pltpu.SMEM),
            pl.BlockSpec(memory_space=pltpu.VMEM),
        ],
        out_specs=pl.BlockSpec(memory_space=pltpu.VMEM),
        scratch_shapes=[
            pltpu.VMEM((nodes, orbits, width), F32),
            pltpu.VMEM((nodes, width, columns), F32),
            pltpu.VMEM((nodes,) + square, F32),
            pltpu.VMEM((nodes,) + square, F32),
            pltpu.VMEM((nodes,) + square, F32),
            pltpu.VMEM((nodes, width, columns), F32),
            pltpu.VMEM((slabs - 1,) + square, F32),
            pltpu.VMEM((slabs - 1,) + square, F32),
            pltpu.VMEM((fills,) + square, F32),
            pltpu.VMEM((fills,) + square, F32),
            pltpu.VMEM((nodes, width, columns), F32),
        ],
        compiler_params=pltpu.CompilerParams(vmem_limit_bytes=VMEM_LIMIT),
        name="solve_slabs",
    )(first, data)


def correlate_kernel(order, got_ref, out_ref):
    count = len(order)
    window = 8
    scale = 1.0 / count
    for start in range(0, count, window):
        span = min(window, count - start)
        acc_re = [None] * span
        acc_im = [None] * span
        reach = count - start
        lead = {}
        for energy in range(reach):
            sender, place = order[energy]
            power = got_ref[sender, 2, place, 0]
            for w in range(span):
                at = energy + start + w
                if at >= count:
                    continue
                if at not in lead:
                    s2, p2 = order[at]
                    lead[at] = (got_ref[s2, 0, p2, 0], got_ref[s2, 1, p2, 0])
                re, im = lead[at]
                acc_re[w] = re * power if acc_re[w] is None else acc_re[w] + re * power
                acc_im[w] = im * power if acc_im[w] is None else acc_im[w] + im * power
        for w in range(span):
            out_ref[0, start + w, 0] = acc_re[w] * scale
            out_ref[1, start + w, 0] = acc_im[w] * scale


def correlate(got, order):
    senders, kinds, mine, per, rows, columns = got.shape
    count = len(order)
    return pl.pallas_call(
        functools.partial(correlate_kernel, order),
        grid=(per,),
        out_shape=jax.ShapeDtypeStruct((2, count, per, rows, columns), F32),
        in_specs=[pl.BlockSpec((senders, kinds, mine, 1, rows, columns), lambda i: (0, 0, 0, i, 0, 0))],
        out_specs=pl.BlockSpec((2, count, 1, rows, columns), lambda i: (0, 0, i, 0, 0)),
        compiler_params=pltpu.CompilerParams(vmem_limit_bytes=VMEM_LIMIT),
        name="correlate",
    )(got)


def per_device(link_p, link_q, shift, lesser_gain, sources):
    per, _, orbits, _ = link_p.shape
    width = 2 * orbits
    columns = sources.shape[-1]
    local = shift.shape[0]
    groups = lax.axis_size("slab")
    energy_groups = lax.axis_size("energy")
    slabs = per * groups
    mine = max(1, local // groups)
    owner = lax.axis_index("slab")
    packed = jnp.concatenate(
        [
            jnp.concatenate([link_p[:, 0], link_p[:, 1]], axis=-1),
            jnp.concatenate([link_q[:, 0], link_q[:, 1]], axis=-1),
            sources.reshape(per, width, columns),
            jnp.swapaxes(jnp.concatenate([shift, lesser_gain], axis=-1), 0, 1),
        ],
        axis=1,
    )
    data = lax.all_gather(packed, "slab", axis=0, tiled=True)
    first = (owner * local // groups).astype(jnp.int32).reshape(1)
    plan = (slabs, mine, orbits, groups, energy_groups, per, orbits // energy_groups)
    sent = solve_slabs(first, data, plan)
    sent = sent.reshape((groups * energy_groups,) + sent.shape[2:])
    got = lax.all_to_all(sent, ("slab", "energy"), split_axis=0, concat_axis=0, tiled=True)
    order = []
    for group in range(energy_groups):
        for row in range(local):
            if local >= groups:
                holder, place = row // mine, row % mine
            else:
                holder, place = -(-row * groups // local), 0
            order.append((holder * energy_groups + group, place))
    return correlate(got, tuple(order))


def solution(mesh):
    placed = (
        P("slab", None, None, None),
        P("slab", None, None, None),
        P("energy", "slab", None),
        P("energy", "slab", None),
        P("slab", None, None, None),
    )
    return jax.shard_map(
        per_device,
        mesh=mesh,
        in_specs=placed,
        out_specs=P(None, None, "slab", "energy", None),
        check_vma=False,
    )
```

time: 1970 us -> 249 us (0.13)
  other arithmetic: 1620 us -> 2.6 us
  Pallas kernels: 0 us -> 137 us
  matrix products: 129 us -> 0 us
  waiting for transfers between devices: 115 us -> 34.2 us
  local copies, waits for them, and re-layouts: 49.9 us -> 1.06 us
  blocking collectives: 21.6 us -> 60.4 us
    another operation x48 -> x0, other arithmetic: 1590 us -> none  [the longest x25 766 us: chain_factor(): factor = jnp.linalg.cholesky(current)]
    pallas_call x0 -> x2, Pallas kernels: none -> 137 us  [the longest x1 130 us: solve_slabs(): pl.pallas_call(functools.partial(kernel_body, plan), out_shape=jax.ShapeD...]
    dot_general x59 -> x0, matrix products: 71.1 us -> none  [the longest x28 39.4 us: left_transposed(): return jnp.einsum('...ji,...jk->...ik', left, right, precision=HIGHEST)]
    all_to_all x0 -> x1, blocking collectives: none -> 60.4 us  [per_device(): lax.all_to_all(sent, ('slab', 'energy'), split_axis=0, concat_axis=0, til...]
    another operation x50 -> x0, matrix products: 57.9 us -> none  [solve_with(): return jax.scipy.linalg.cho_solve((factor, True), rhs)]
    all_to_all x3 -> x0, waiting for transfers between devices: 51.8 us -> none  [the longest x1 19.6 us: per_device(): lax.all_to_all(elem_re, 'energy', split_axis=2, concat_axis=1, tiled=True)]
    all_gather x7 -> x1, waiting for transfers between devices: 62.8 us -> 34.2 us  [per_device(): data = lax.all_gather(packed, 'slab', axis=0, tiled=True)]
    unnamed x246 -> x0, local copies, waits for them, and re-layouts: 22.4 us -> none
  transfers between devices with their start and end apart: 10 -> 1, of which waited for: 5 -> 1; matrix products, arithmetic and copies ran while one was open for 78% -> 0% of each run, Pallas kernels for 0% -> 0%
where the time goes in v1:
time: 249 us
  Pallas kernels  137 us (55%)
  blocking collectives  60.4 us (24%)
  waiting for transfers between devices  34.2 us (14%)
  between operations  13.4 us (5%)
  other arithmetic  2.6 us (1%)
    pallas_call x1, Pallas kernels, solve_slabs(): pl.pallas_call(functools.partial(kernel_body, plan), out_shape=jax.ShapeD...  130 us
    all_to_all x1, blocking collectives, per_device(): lax.all_to_all(sent, ('slab', 'energy'), split_axis=0, concat_axis=0, til...  60.4 us
    all_gather x1, waiting for transfers between devices, per_device(): data = lax.all_gather(packed, 'slab', axis=0, tiled=True)  34.2 us
    pallas_call x1, Pallas kernels, correlate(): pl.pallas_call(functools.partial(correlate_kernel, order), grid=(per,), o...  7.08 us
  transfers between devices with their start and end apart: 1, of which 1 were waited for; matrix products, arithmetic and copies ran while one was open for 0% of the time, Pallas kernels for 0%

profile of v1, /device:TPU:0, one launch (start us, length us, event | category | flops | bytes accessed | tf_op | source)
XLA Modules:
  0.0 248.8 jit_solution(6685417083366879823)
XLA Ops:
  6.5 0.0 all-gather.2.cloned.1.call-start
  6.5 0.8 maximum_bitcast_fusion
  7.3 1.1 slice_bitcast_fusion.1
  8.4 1.8 pad_maximum_fusion
  10.2 0.0 all-gather.2.cloned.1.call-update
  10.2 34.2 %all-gather.2.cloned.1.call-done.data_ref = f32[12,264,128]{2,1,0:T(8,128)} async-done(((f32[3,264,128]{2,1,0:T(8,128)}), f32[12,264,128]{2,1,0:T(8,128)}) %all-gather.2.cloned.1.call-update) | async-done | bytes 1622032 | tf_op jit(solution)/shard_map/all_gather | solution.py:386
  44.5 130.0 %solve_slabs.1 = f32[4,8,3,2,3,8,128]{6,5,4,3,2,1,0:T(8,128)} custom-call(s32[1]{0:T(128)} %bitcast.first_ref, f32[12,264,128]{2,1,0:T(8,128)} %all-gather.2.cloned.1.call-done.data_ref), custom_call_target="tpu_custom_call" | custom-call | tf_op jit(solution)/shard_map/solve_slabs/pallas_call | solution.py:299
  174.5 60.4 %all_to_all.5.got_ref = f32[32,3,2,3,8,128]{5,4,3,2,1,0:T(8,128)} all-to-all(f32[32,3,2,3,8,128]{5,4,3,2,1,0:T(8,128)} %bitcast.21), channel_id=1, replica_groups=mesh['slab'=4,'energy'=8] {'slab','energy'}, dimensions={0} | all-to-all | bytes 4718592 | tf_op jit(solution)/shard_map/all_to_all | solution.py:391
  234.8 7.1 %correlate.1 = f32[2,64,3,8,128]{4,3,2,1,0:T(8,128)} custom-call(f32[32,3,2,3,8,128]{5,4,3,2,1,0:T(8,128)} %all_to_all.5.got_ref), custom_call_target="tpu_custom_call" | custom-call | tf_op jit(solution)/shard_map/correlate/pallas_call | solution.py:356
Async XLA Ops:
  6.5 37.9 %all-gather.2.cloned.1.call-start = ((), (), s32[]{:S(2)}) async-start(), calls=%async_computation.1 | async-start | bytes 2027520 | tf_op jit(solution)/shard_map/all_gather | solution.py:386
Sparse Core Ops, SparseCore 0:
  10.4 34.0 all-gather.1

commit v2 on v1

v2 whole, which is shorter than its diff:
```python
import functools

import jax
import jax.numpy as jnp
from jax import lax
from jax.experimental import pallas as pl
from jax.experimental.pallas import tpu as pltpu
from jax.sharding import PartitionSpec as P

F32 = jnp.float32
BF16 = jnp.bfloat16
VMEM_LIMIT = 56 * 1024 * 1024
PANEL = 8
BROADCAST_UP_TO = 6


def elimination_levels(count):
    levels = []
    chain = list(range(count))
    while len(chain) > 1:
        level = []
        for place in range(0, len(chain), 2):
            left = chain[place - 1] if place > 0 else None
            right = chain[place + 1] if place + 1 < len(chain) else None
            level.append((chain[place], left, right))
        levels.append(level)
        chain = chain[1::2]
    return levels, chain[0]


def thirds(x):
    one = x.astype(BF16)
    rest = x - one.astype(F32)
    two = rest.astype(BF16)
    three = (rest - two.astype(F32)).astype(BF16)
    return one, two, three


def mm(a, b):
    a1, a2, a3 = thirds(a)
    b1, b2, b3 = thirds(b)
    left = jnp.concatenate([a1, a2, a1, a2, a1, a3], axis=1)
    right = jnp.concatenate([b1, b1, b2, b2, b3, b1], axis=0)
    return lax.dot_general(left, right, (((1,), (0,)), ((), ())), preferred_element_type=F32)


def mm_nt(a, b):
    a1, a2, a3 = thirds(a)
    b1, b2, b3 = thirds(b)
    left = jnp.concatenate([a1, a2, a1, a2, a1, a3], axis=1)
    right = jnp.concatenate([b1, b1, b2, b2, b3, b1], axis=1)
    return lax.dot_general(left, right, (((1,), (1,)), ((), ())), preferred_element_type=F32)


def half_roll(x):
    return pltpu.roll(x, x.shape[1] // 2, 1)


def invert_batch(mat_ref, members, orbits):
    width = 2 * orbits
    blocks = orbits // PANEL
    lane = lax.broadcasted_iota(jnp.int32, (PANEL, width), 1)
    sub = lax.broadcasted_iota(jnp.int32, (PANEL, width), 0)
    pivots = (lane < PANEL) | ((lane >= orbits) & (lane < orbits + PANEL))

    def panel(p, unused):
        rows = pl.ds(pl.multiple_of(p * PANEL, PANEL), PANEL)
        original = lax.rem(lane + p * PANEL, width)
        sign = jnp.where(original < orbits, -1.0, 1.0).astype(F32)
        tops = []
        for m in members:
            tops.append(mat_ref[m, rows, :])
        hats = []
        if len(members) > BROADCAST_UP_TO:
            for k in range(PANEL):
                here = sub == k
                at_pivot = (lane == k) | (lane == orbits + k)
                unit = jnp.where(here & (lane == k), 1.0, 0.0).astype(F32)
                for n in range(len(tops)):
                    r = tops[n]
                    cr = jnp.broadcast_to(r[:, k : k + 1], r.shape)
                    ci = jnp.broadcast_to(r[:, orbits + k : orbits + k + 1], r.shape)
                    inv = 1.0 / cr[k : k + 1, :]
                    r0 = jnp.where(at_pivot, unit, r)
                    row = r0[k : k + 1, :] * inv
                    hat = half_roll(r0)[k : k + 1, :] * (sign[k : k + 1, :] * inv)
                    tops[n] = jnp.where(here, row, r0 - cr * row - ci * hat)
            for r in tops:
                hats.append(half_roll(r) * sign)
        else:
            eye = jnp.where(lane == sub, 1.0, 0.0).astype(F32)
            turned = jnp.where(lane == sub + orbits, 1.0, 0.0).astype(F32) * sign
            cols = []
            for n in range(len(tops)):
                r = tops[n]
                cols.append(
                    [
                        (
                            jnp.broadcast_to(r[:, j : j + 1], r.shape),
                            jnp.broadcast_to(r[:, orbits + j : orbits + j + 1], r.shape),
                        )
                        for j in range(PANEL)
                    ]
                )
                hats.append(jnp.where(pivots, turned, half_roll(r) * sign))
                tops[n] = jnp.where(pivots, eye, r)
            for k in range(PANEL):
                here = sub == k
                for n in range(len(tops)):
                    r, hat = tops[n], hats[n]
                    cr, ci = cols[n][k]
                    inv = 1.0 / cr[k : k + 1, :]
                    ur, ui = cr * inv, ci * inv
                    for j in range(k + 1, PANEL):
                        er, ei = cols[n][j]
                        fr, fi = er[k : k + 1, :], ei[k : k + 1, :]
                        cols[n][j] = (
                            jnp.where(here, fr * inv, er - ur * fr + ui * fi),
                            jnp.where(here, fi * inv, ei - ur * fi - ui * fr),
                        )
                    row, hat_row = r[k : k + 1, :], hat[k : k + 1, :]
                    tops[n] = jnp.where(here, row * inv, r - ur * row - ui * hat_row)
                    hats[n] = jnp.where(here, hat_row * inv, hat - ur * hat_row + ui * row)
        for n, m in enumerate(members):
            r, hat = tops[n], hats[n]
            for i in range(blocks):
                block = mat_ref[m, PANEL * i : PANEL * (i + 1), :]
                out = jnp.where(pivots, 0.0, block)
                for j in range(PANEL):
                    out = out - jnp.broadcast_to(block[:, j : j + 1], out.shape) * r[j : j + 1, :]
                    out = out - jnp.broadcast_to(block[:, orbits + j : orbits + j + 1], out.shape) * hat[j : j + 1, :]
                mat_ref[m, PANEL * i : PANEL * (i + 1), :] = pltpu.roll(out, width - PANEL, 1)
            mat_ref[m, rows, :] = pltpu.roll(r, width - PANEL, 1)
        return 0

    lax.fori_loop(0, blocks, panel, 0)


def link_places(slabs, mine, levels):
    places = {}
    for s in range(slabs - 1):
        for e in range(mine):
            places[(0, s, s + 1, e)] = (True, s)
    spare = 0
    for depth, level in enumerate(levels):
        for node, left, right in level:
            if left is not None and right is not None:
                for e in range(mine):
                    places[(depth + 1, left, right, e)] = (False, spare)
                    spare += 1
    return places, spare


def climb(levels, mine, w1, w2, sol):
    for level in reversed(levels):
        for node, left, right in level:
            for e in range(mine):
                m = node * mine + e
                if left is not None and right is not None:
                    both = jnp.concatenate([w1[m], w2[m]], axis=1)
                    sides = jnp.concatenate([sol[left * mine + e], sol[right * mine + e]], axis=0)
                    sol[m] = sol[m] - mm(both, sides)
                elif left is not None:
                    sol[m] = sol[m] - mm(w1[m], sol[left * mine + e])
                elif right is not None:
                    sol[m] = sol[m] - mm(w2[m], sol[right * mine + e])


def retarded_kernel(plan, where_ref, *refs):
    (slabs, mine, orbits, groups, energy_groups, per, orb_per) = plan
    pq_ref, src_ref, set_ref = refs[0], refs[1], refs[2]
    peers = refs[3 : 3 + 2 * (groups - 1)]
    power_ref, inv, w1, w2, up1, dn1, up2, dn2, sol, gains, data, mat, rhs = refs[3 + 2 * (groups - 1) :]
    width = 2 * orbits
    levels, root = elimination_levels(slabs)
    places, _ = link_places(slabs, mine, levels)
    lane = lax.broadcasted_iota(jnp.int32, (orbits, width), 1)
    sub = lax.broadcasted_iota(jnp.int32, (orbits, width), 0)
    low = lane < orbits
    low_all = lax.broadcasted_iota(jnp.int32, (width, width), 1) < orbits
    diag_lane = lane == sub
    first, owner, core = where_ref[0], where_ref[1], where_ref[2]

    local = set_ref.shape[1]
    for i in range(per):
        at = owner * per + i
        data[at, 0:width, :] = pq_ref[i]
        data[at, width : 2 * width, :] = src_ref[i]
        data[at, 2 * width : 2 * width + local, :] = set_ref[i]
    for k in range(1, groups):
        mine_half, other_half = peers[2 * (k - 1)], peers[2 * (k - 1) + 1]
        for i in range(per):
            at = (owner ^ k) * per + i
            data[at, pl.ds(pl.multiple_of(core * width, width), width), :] = mine_half[i, 0:width, :]
            data[at, pl.ds(pl.multiple_of((1 - core) * width, width), width), :] = other_half[i, 0:width, :]
            data[at, 2 * width : 2 * width + local, :] = mine_half[i, width : width + local, :]

    def real_rows(z):
        return jnp.concatenate([jnp.where(low, z, -z), half_roll(z)], axis=0)

    def trans_rows(z):
        return jnp.concatenate([z, jnp.where(low, -half_roll(z), half_roll(z))], axis=0)

    def real_left(t):
        top, bottom = t[:orbits], t[orbits:]
        return jnp.concatenate(
            [jnp.where(low, top, -half_roll(bottom)), jnp.where(low, bottom, half_roll(top))], axis=0
        )

    def real_right(t):
        top, bottom = t[:orbits], t[orbits:]
        return jnp.concatenate(
            [jnp.where(low, half_roll(top), -bottom), jnp.where(low, half_roll(bottom), top)], axis=0
        )

    def packed_left(t):
        return jnp.where(low, t[:orbits], half_roll(t[orbits:]))

    def packed_right(t):
        return jnp.where(low, half_roll(t[:orbits]), t[orbits:])

    def factor_p(s):
        return data[s, 0:orbits, :]

    def factor_q(s):
        return data[s, orbits : 2 * orbits, :]

    for s in range(slabs):
        zq = factor_q(s)
        base = mm_nt(zq, trans_rows(zq))
        if s + 1 < slabs:
            zp = factor_p(s + 1)
            base = base + mm_nt(zp, trans_rows(zp))
            rp = real_rows(zp)
            rq = real_rows(factor_q(s + 1))
            up1[s] = -mm_nt(rp, rq)
            dn1[s] = -mm_nt(rq, rp)
        if s == 0:
            zp = factor_p(0)
            base = base + mm_nt(zp, trans_rows(zp))
        for e in range(mine):
            settings = data[s, pl.ds(2 * width + first + e, 1), :]
            gains[s * mine + e] = settings
            mat[s * mine + e] = base + jnp.where(diag_lane, settings, 0.0)
            rhs[s * mine + e] = data[s, width : 2 * width, :]

    def held(key):
        basic, place = places[key]
        return (up1, dn1, place) if basic else (up2, dn2, place)

    def couplings(depth, node, left, right, e):
        if left is None:
            to_left = 0.0
        else:
            _, downs, place = held((depth, left, node, e))
            to_left = downs[place]
        if right is None:
            to_right = 0.0
        else:
            ups, _, place = held((depth, node, right, e))
            to_right = half_roll(ups[place])
        return jnp.where(low_all, to_left, to_right)

    for depth, level in enumerate(levels):
        invert_batch(mat, [node * mine + e for node, _, _ in level for e in range(mine)], orbits)
        for node, left, right in level:
            for e in range(mine):
                m = node * mine + e
                full = real_rows(half_roll(mat[m]))
                inv[m] = full
                stacked = jnp.concatenate([couplings(depth, node, left, right, e), rhs[m]], axis=1)
                step = mm(full, stacked)
                links_step, rhs_step = step[:, :width], step[:, width:]
                sol[m] = rhs_step
                if left is not None:
                    w1[m] = real_left(links_step)
                    ups, _, place = held((depth, left, node, e))
                    change = mm(ups[place], step)
                    ml = left * mine + e
                    mat[ml] = mat[ml] - packed_left(change[:, :width])
                    rhs[ml] = rhs[ml] - change[:, width:]
                    if right is not None:
                        ups, _, place = held((depth + 1, left, right, e))
                        ups[place] = -real_right(change[:, :width])
                if right is not None:
                    w2[m] = real_right(links_step)
                    _, downs, place = held((depth, node, right, e))
                    change = mm(downs[place], step)
                    mr = right * mine + e
                    mat[mr] = mat[mr] - packed_right(change[:, :width])
                    rhs[mr] = rhs[mr] - change[:, width:]
                    if left is not None:
                        _, downs, place = held((depth + 1, left, right, e))
                        downs[place] = -real_left(change[:, :width])
    invert_batch(mat, [root * mine + e for e in range(mine)], orbits)
    for e in range(mine):
        m = root * mine + e
        full = real_rows(half_roll(mat[m]))
        inv[m] = full
        sol[m] = mm(full, rhs[m])
    climb(levels, mine, w1, w2, sol)
    for s in range(slabs):
        for e in range(mine):
            x = sol[s * mine + e]
            xr, xi = x[:orbits], x[orbits:]
            power = xr * xr + xi * xi
            for j in range(energy_groups):
                power_ref[s // per, j, e, s % per, :, :] = power[j * orb_per : (j + 1) * orb_per, :]


def lesser_kernel(plan, inv, w1, w2, up1, dn1, up2, dn2, ret, gains, out_ref, rhs, sol):
    (slabs, mine, orbits, groups, energy_groups, per, orb_per) = plan
    width = 2 * orbits
    levels, root = elimination_levels(slabs)
    places, _ = link_places(slabs, mine, levels)
    lane = lax.broadcasted_iota(jnp.int32, (orbits, width), 1)
    sub = lax.broadcasted_iota(jnp.int32, (orbits, width), 0)
    gain_lane = lane == sub + orbits
    for m in range(slabs * mine):
        gain = jnp.sum(jnp.where(gain_lane, gains[m], 0.0), axis=1, keepdims=True)
        rhs[m] = ret[m] * jnp.concatenate([gain, gain], axis=0)
    for depth, level in enumerate(levels):
        for node, left, right in level:
            for e in range(mine):
                m = node * mine + e
                step = mm(inv[m], rhs[m])
                sol[m] = step
                if left is not None:
                    basic, place = places[(depth, left, node, e)]
                    ml = left * mine + e
                    rhs[ml] = rhs[ml] - mm((up1 if basic else up2)[place], step)
                if right is not None:
                    basic, place = places[(depth, node, right, e)]
                    mr = right * mine + e
                    rhs[mr] = rhs[mr] - mm((dn1 if basic else dn2)[place], step)
    for e in range(mine):
        m = root * mine + e
        sol[m] = mm(inv[m], rhs[m])
    climb(levels, mine, w1, w2, sol)
    for s in range(slabs):
        for e in range(mine):
            m = s * mine + e
            x, y = ret[m], sol[m]
            xr, xi, yr, yi = x[:orbits], x[orbits:], y[:orbits], y[orbits:]
            re = xr * yr + xi * yi
            im = xr * yi - xi * yr
            for j in range(energy_groups):
                rows = slice(j * orb_per, (j + 1) * orb_per)
                out_ref[s // per, j, 0, e, s % per, :, :] = re[rows, :]
                out_ref[s // per, j, 1, e, s % per, :, :] = im[rows, :]


def vmem_specs(count):
    return [pl.BlockSpec(memory_space=pltpu.VMEM)] * count


def solve_retarded(where, pieces, plan, columns):
    (slabs, mine, orbits, groups, energy_groups, per, orb_per) = plan
    width = 2 * orbits
    nodes = slabs * mine
    levels, _ = elimination_levels(slabs)
    _, fills = link_places(slabs, mine, levels)
    local = pieces[2].shape[1]
    shapes = [
        (groups, energy_groups, mine, per, orb_per, columns),
        (nodes, width, width),
        (nodes, width, width),
        (nodes, width, width),
        (slabs - 1, width, width),
        (slabs - 1, width, width),
        (fills, width, width),
        (fills, width, width),
        (nodes, width, columns),
        (nodes, 1, width),
    ]
    return pl.pallas_call(
        functools.partial(retarded_kernel, plan),
        out_shape=[jax.ShapeDtypeStruct(shape, F32) for shape in shapes],
        in_specs=[pl.BlockSpec(memory_space=pltpu.SMEM)] + vmem_specs(len(pieces)),
        out_specs=vmem_specs(len(shapes)),
        scratch_shapes=[
            pltpu.VMEM((slabs, 2 * width + local, columns), F32),
            pltpu.VMEM((nodes, orbits, width), F32),
            pltpu.VMEM((nodes, width, columns), F32),
        ],
        compiler_params=pltpu.CompilerParams(vmem_limit_bytes=VMEM_LIMIT),
        name="solve_retarded",
    )(where, *pieces)


def solve_lesser(stored, plan):
    (slabs, mine, orbits, groups, energy_groups, per, orb_per) = plan
    solved = stored[7].shape
    return pl.pallas_call(
        functools.partial(lesser_kernel, plan),
        out_shape=jax.ShapeDtypeStruct((groups, energy_groups, 2, mine, per, orb_per, solved[-1]), F32),
        in_specs=vmem_specs(len(stored)),
        out_specs=pl.BlockSpec(memory_space=pltpu.VMEM),
        scratch_shapes=[pltpu.VMEM(solved, F32), pltpu.VMEM(solved, F32)],
        compiler_params=pltpu.CompilerParams(vmem_limit_bytes=VMEM_LIMIT),
        name="solve_lesser",
    )(*stored)


def correlate_kernel(order, power_ref, got_ref, out_ref):
    count = len(order)
    window = 8
    scale = 1.0 / count
    for start in range(0, count, window):
        span = min(window, count - start)
        acc_re = [None] * span
        acc_im = [None] * span
        reach = count - start
        lead = {}
        for energy in range(reach):
            sender, place = order[energy]
            power = power_ref[sender, place, 0]
            for w in range(span):
                at = energy + start + w
                if at >= count:
                    continue
                if at not in lead:
                    s2, p2 = order[at]
                    lead[at] = (got_ref[s2, 0, p2, 0], got_ref[s2, 1, p2, 0])
                re, im = lead[at]
                acc_re[w] = re * power if acc_re[w] is None else acc_re[w] + re * power
                acc_im[w] = im * power if acc_im[w] is None else acc_im[w] + im * power
        for w in range(span):
            out_ref[0, start + w, 0] = acc_re[w] * scale
            out_ref[1, start + w, 0] = acc_im[w] * scale


def correlate(power, got, order):
    senders, kinds, mine, per, rows, columns = got.shape
    count = len(order)
    return pl.pallas_call(
        functools.partial(correlate_kernel, order),
        grid=(per,),
        out_shape=jax.ShapeDtypeStruct((2, count, per, rows, columns), F32),
        in_specs=[
            pl.BlockSpec((senders, mine, 1, rows, columns), lambda i: (0, 0, i, 0, 0)),
            pl.BlockSpec((senders, kinds, mine, 1, rows, columns), lambda i: (0, 0, 0, i, 0, 0)),
        ],
        out_specs=pl.BlockSpec((2, count, 1, rows, columns), lambda i: (0, 0, i, 0, 0)),
        compiler_params=pltpu.CompilerParams(vmem_limit_bytes=VMEM_LIMIT),
        name="correlate",
    )(power, got)


def per_device(link_p, link_q, shift, lesser_gain, sources):
    per, _, orbits, _ = link_p.shape
    width = 2 * orbits
    columns = sources.shape[-1]
    local = shift.shape[0]
    groups = lax.axis_size("slab")
    energy_groups = lax.axis_size("energy")
    slabs = per * groups
    mine = max(1, local // groups)
    owner = lax.axis_index("slab")
    factors = jnp.concatenate(
        [
            jnp.concatenate([link_p[:, 0], link_p[:, 1]], axis=-1),
            jnp.concatenate([link_q[:, 0], link_q[:, 1]], axis=-1),
        ],
        axis=1,
    )
    columns_in = sources.reshape(per, width, columns)
    settings = jnp.swapaxes(jnp.concatenate([shift, lesser_gain], axis=-1), 0, 1)
    place = lax.axis_index("energy")
    core = place % 2
    parcel = jnp.concatenate([jnp.where(core == 0, factors, columns_in), settings], axis=1)
    siblings = [(j, j ^ 1) for j in range(energy_groups)]
    pieces = [factors, columns_in, settings]
    fetched = [lax.ppermute(parcel, "slab", [(g, g ^ k) for g in range(groups)]) for k in range(1, groups)]
    for piece in fetched:
        pieces.append(piece)
        pieces.append(lax.ppermute(piece, "energy", siblings))
    where = jnp.stack([owner * local // groups, owner, core]).astype(jnp.int32)
    plan = (slabs, mine, orbits, groups, energy_groups, per, orbits // energy_groups)
    power, *stored = solve_retarded(where, pieces, plan, columns)

    def spread(array):
        array = array.reshape((groups * energy_groups,) + array.shape[2:])
        return lax.all_to_all(array, ("slab", "energy"), split_axis=0, concat_axis=0, tiled=True)

    power = spread(power)
    got = spread(solve_lesser(stored, plan))
    order = []
    for group in range(energy_groups):
        for row in range(local):
            if local >= groups:
                holder, place = row // mine, row % mine
            else:
                holder, place = -(-row * groups // local), 0
            order.append((holder * energy_groups + group, place))
    return correlate(power, got, tuple(order))


def solution(mesh):
    placed = (
        P("slab", None, None, None),
        P("slab", None, None, None),
        P("energy", "slab", None),
        P("energy", "slab", None),
        P("slab", None, None, None),
    )
    return jax.shard_map(
        per_device,
        mesh=mesh,
        in_specs=placed,
        out_specs=P(None, None, "slab", "energy", None),
        check_vma=False,
    )
```

time: 249 us -> 240 us (0.964)
  Pallas kernels: 137 us -> 164 us
  blocking collectives: 60.4 us -> 42.2 us
  waiting for transfers between devices: 34.2 us -> 18 us
  between operations: 13.4 us -> 0.05 us
  starting transfers between devices: 0.01 us -> 10.2 us
    all_gather x1 -> x0, waiting for transfers between devices: 34.2 us -> none  [per_device(): data = lax.all_gather(packed, 'slab', axis=0, tiled=True)]
    pallas_call x1 -> x2, Pallas kernels: 130 us -> 157 us  [the longest x1 144 us: solve_retarded(): pl.pallas_call(functools.partial(retarded_kernel, plan), out_shape=[jax.S...]
    all_to_all x1, blocking collectives: 60.4 us -> 42.2 us  [spread(): lax.all_to_all(array, ('slab', 'energy'), split_axis=0, concat_axis=0, ti...]
    ppermute x0 -> x6, waiting for transfers between devices: none -> 9.84 us  [the longest x3 9.27 us: per_device(): lax.ppermute(parcel, 'slab', [(g, g ^ k) for g in range(groups)])]
    all_to_all x0 -> x1, waiting for transfers between devices: none -> 8.2 us  [spread(): lax.all_to_all(array, ('slab', 'energy'), split_axis=0, concat_axis=0, ti...]
    all_to_all x0 -> x1, starting transfers between devices: none -> 5.33 us  [spread(): lax.all_to_all(array, ('slab', 'energy'), split_axis=0, concat_axis=0, ti...]
    ppermute x0 -> x6, starting transfers between devices: none -> 4.84 us  [the longest x3 4.6 us: per_device(): lax.ppermute(parcel, 'slab', [(g, g ^ k) for g in range(groups)])]
  transfers between devices with their start and end apart: 1 -> 7, of which waited for: 1 -> 6; matrix products, arithmetic and copies ran while one was open for 0% -> 0% of each run, Pallas kernels for 0% -> 6%
where the time goes in v2:
time: 240 us
  Pallas kernels  164 us (68%)
  blocking collectives  42.2 us (18%)
  waiting for transfers between devices  18 us (8%)
  starting transfers between devices  10.2 us (4%)
  other arithmetic  3.2 us (1%)
    pallas_call x1, Pallas kernels, solve_retarded(): pl.pallas_call(functools.partial(retarded_kernel, plan), out_shape=[jax.S...  144 us
    all_to_all x1, blocking collectives, spread(): lax.all_to_all(array, ('slab', 'energy'), split_axis=0, concat_axis=0, ti...  42.2 us
    pallas_call x1, Pallas kernels, solve_lesser(): pl.pallas_call(functools.partial(lesser_kernel, plan), out_shape=jax.Shap...  13.8 us
    ppermute x3, waiting for transfers between devices, per_device(): lax.ppermute(parcel, 'slab', [(g, g ^ k) for g in range(groups)])  9.27 us
    all_to_all x1, waiting for transfers between devices, spread(): lax.all_to_all(array, ('slab', 'energy'), split_axis=0, concat_axis=0, ti...  8.2 us
    pallas_call x1, Pallas kernels, correlate(): pl.pallas_call(functools.partial(correlate_kernel, order), grid=(per,), o...  7.08 us
    all_to_all x1, starting transfers between devices, spread(): lax.all_to_all(array, ('slab', 'energy'), split_axis=0, concat_axis=0, ti...  5.33 us
  transfers between devices with their start and end apart: 7, of which 6 were waited for; matrix products, arithmetic and copies ran while one was open for 0% of the time, Pallas kernels for 6%

profile of v2, /device:TPU:0, one launch (start us, length us, event | category | flops | bytes accessed | tf_op | source)
XLA Modules:
  0.0 239.8 jit_solution(8948876143584907240)
XLA Ops:
  0.0 0.8 maximum_bitcast_fusion.refs_2_
  0.8 0.0 copy-start.7
  0.8 1.1 slice_bitcast_fusion.1
  1.9 1.7 broadcast_select_fusion
  3.6 4.0 %collective-permute-start.4 = (f32[3,136,128]{2,1,0:T(8,128)S(1)}, f32[3,136,128]{2,1,0:T(8,128)S(1)}, u32[]{:S(2)}, u32[]{:S(2)}) collective-permute-start(f32[3,136,128]{2,1,0:T(8,128)S(1)} %pad_maximum_fusion), channel_id=1, source_target_pairs={{0,24},{8,16},{16,8},{24,0},{1,25},{9,17},{17,9},{25,1},{2,26},{10... | collective-permute-start | bytes 626696 | tf_op jit(solution)/shard_map/ppermute | solution.py:474
  7.6 0.5 collective-permute-start.2
  8.1 0.1 collective-permute-start
  8.2 5.4 %collective-permute-done.4.refs_7_ = f32[3,136,128]{2,1,0:T(8,128)S(1)} collective-permute-done((f32[3,136,128]{2,1,0:T(8,128)S(1)}, f32[3,136,128]{2,1,0:T(8,128)S(1)}, u32[]{:S(2)}, u32[]{:S(2)}) %collective-permute-start.4) | collective-permute-done | bytes 208928 | tf_op jit(solution)/shard_map/ppermute | solution.py:474
  13.6 0.0 copy-start.1
  13.6 0.0 collective-permute-start.5
  13.6 3.6 %collective-permute-done.2.refs_5_ = f32[3,136,128]{2,1,0:T(8,128)S(1)} collective-permute-done((f32[3,136,128]{2,1,0:T(8,128)S(1)}, f32[3,136,128]{2,1,0:T(8,128)S(1)}, u32[]{:S(2)}, u32[]{:S(2)}) %collective-permute-start.2) | collective-permute-done | bytes 208928 | tf_op jit(solution)/shard_map/ppermute | solution.py:474
  17.2 0.0 collective-permute-start.3
  17.2 0.3 collective-permute-done.refs_3_
  17.5 0.2 collective-permute-start.1
  17.7 0.7 pad_add_fusion.where_ref
  18.4 0.0 collective-permute-done.5.refs_8_
  18.4 0.3 collective-permute-done.3.refs_6_
  18.7 0.3 collective-permute-done.1.refs_4_
  19.0 0.0 copy-done.7
  19.0 0.0 copy-done.1
  19.0 0.0 copy-done.2
  19.0 0.0 copy-done.3
  19.0 0.1 copy-done.4
  19.1 0.3 copy-done.5
  19.4 0.3 copy-done.6
  19.7 143.5 %solve_retarded.1 = (f32[4,8,2,3,8,128]{5,4,3,2,1,0:T(8,128)}, f32[24,128,128]{2,1,0:T(8,128)}, f32[24,128,128]{2,1,0:T(8,128)}, f32[24,128,128]{2,1,0:T(8,128)}...) custom-call(s32[3]{0:T(128)} %pad_add_fusion.where_ref, ...), custom_call_target="tpu_custom_call" | custom-call | tf_op jit(solution)/shard_map/solve_retarded/pallas_call | solution.py:376
  163.2 5.3 %all-to-all-start = ((f32[32,2,3,8,128]{4,3,2,1,0:T(8,128)}), f32[32,2,3,8,128]{4,3,2,1,0:T(8,128)S(1)}, u32[]{:S(2)}, u32[]{:S(2)}) async-start(f32[32,2,3,8,128]{4,3,2,1,0:T(8,128)} %bitcast.27), calls=%async_computation | async-start | bytes 1572864 | tf_op jit(solution)/shard_map/all_to_all | solution.py:484
  168.5 13.8 %solve_lesser.1 = f32[4,8,2,2,3,8,128]{6,5,4,3,2,1,0:T(8,128)} custom-call(f32[24,128,128]{2,1,0:T(8,128)} %get-tuple-element.16.inv, f32[24,128,128]{2,1,0:T(8,128)} %get-tuple-element.17.w1, f32[24,128,128]{2,1,0:T(8,128)} %get-tuple-element.18.w2, f32[11,128,128]{2,1,0:T(8,128)} %get-tuple-element.19.up1, f32[11,128,128]{2,1,0:T(8,128)} %get-tuple-element.20.dn1, ...), custom_call_target="tpu_custom_call" | custom-call | tf_op jit(solution)/shard_map/solve_lesser/pallas_call | solution.py:394
  182.3 8.2 %all-to-all-done.power_ref = f32[32,2,3,8,128]{4,3,2,1,0:T(8,128)S(1)} async-done(((f32[32,2,3,8,128]{4,3,2,1,0:T(8,128)}), f32[32,2,3,8,128]{4,3,2,1,0:T(8,128)S(1)}, u32[]{:S(2)}, u32[]{:S(2)}) %all-to-all-start) | async-done | bytes 786464 | tf_op jit(solution)/shard_map/all_to_all | solution.py:484
  190.5 42.2 %all_to_all.10.got_ref = f32[32,2,2,3,8,128]{5,4,3,2,1,0:T(8,128)} all-to-all(f32[32,2,2,3,8,128]{5,4,3,2,1,0:T(8,128)} %bitcast.25), channel_id=1, replica_groups=mesh['slab'=4,'energy'=8] {'slab','energy'}, dimensions={0} | all-to-all | bytes 3145728 | tf_op jit(solution)/shard_map/all_to_all | solution.py:484
  232.7 0.0 copy-done
  232.7 7.1 %correlate.1 = f32[2,64,3,8,128]{4,3,2,1,0:T(8,128)} custom-call(f32[32,2,3,8,128]{4,3,2,1,0:T(8,128)} %copy-done, f32[32,2,2,3,8,128]{5,4,3,2,1,0:T(8,128)} %all_to_all.10.got_ref), custom_call_target="tpu_custom_call" | custom-call | tf_op jit(solution)/shard_map/correlate/pallas_call | solution.py:436
  (7 shorter events, 0.0 us)
Async XLA Ops:
  0.8 18.2 %copy-start.7 = (f32[3,8,128]{2,1,0:T(8,128)}, f32[3,8,128]{2,1,0:T(8,128)S(1)}, u32[]{:S(2)}) copy-start(f32[3,8,128]{2,1,0:T(8,128)S(1)} %maximum_bitcast_fusion.refs_2_) | copy-start | bytes 36868
  3.6 10.0 %collective-permute-start.4 = (f32[3,136,128]{2,1,0:T(8,128)S(1)}, f32[3,136,128]{2,1,0:T(8,128)S(1)}, u32[]{:S(2)}, u32[]{:S(2)}) collective-permute-start(f32[3,136,128]{2,1,0:T(8,128)S(1)} %pad_maximum_fusion), channel_id=1, source_target_pairs={{0,24},{8,16},{16,8},{24,0},{1,25},{9,17},{17,9},{25,1},{2,26},{10... | collective-permute-start | bytes 626696 | tf_op jit(solution)/shard_map/ppermute | solution.py:474
  7.6 9.6 %collective-permute-start.2 = (f32[3,136,128]{2,1,0:T(8,128)S(1)}, f32[3,136,128]{2,1,0:T(8,128)S(1)}, u32[]{:S(2)}, u32[]{:S(2)}) collective-permute-start(f32[3,136,128]{2,1,0:T(8,128)S(1)} %pad_maximum_fusion), channel_id=1, source_target_pairs={{0,16},{8,24},{16,0},{24,8},{1,17},{9,25},{17,1},{25,9},{2,18},{10... | collective-permute-start | bytes 626696 | tf_op jit(solution)/shard_map/ppermute | solution.py:474
  8.1 9.4 %collective-permute-start = (f32[3,136,128]{2,1,0:T(8,128)S(1)}, f32[3,136,128]{2,1,0:T(8,128)S(1)}, u32[]{:S(2)}, u32[]{:S(2)}) collective-permute-start(f32[3,136,128]{2,1,0:T(8,128)S(1)} %pad_maximum_fusion), channel_id=1, source_target_pairs={{0,8},{8,0},{16,24},{24,16},{1,9},{9,1},{17,25},{25,17},{2,10},{10... | collective-permute-start | bytes 626696 | tf_op jit(solution)/shard_map/ppermute | solution.py:474
  13.6 5.4 %copy-start.1 = (f32[3,136,128]{2,1,0:T(8,128)}, f32[3,136,128]{2,1,0:T(8,128)S(1)}, u32[]{:S(2)}) copy-start(f32[3,136,128]{2,1,0:T(8,128)S(1)} %collective-permute-done.4.refs_7_) | copy-start | bytes 626692
  13.6 4.8 %collective-permute-start.5 = (f32[3,136,128]{2,1,0:T(8,128)S(1)}, f32[3,136,128]{2,1,0:T(8,128)S(1)}, u32[]{:S(2)}, u32[]{:S(2)}) collective-permute-start(f32[3,136,128]{2,1,0:T(8,128)S(1)} %collective-permute-done.4.refs_7_), channel_id=1, source_target_pairs={{0,1},{1,0},{2,3},{3,2},{4,5},{5,4},{6,7},{7,6},{8,9},{9,8},{10,11... | collective-permute-start | bytes 626696 | tf_op jit(solution)/shard_map/ppermute | solution.py:477
  17.2 1.8 copy-start.2
  17.2 1.5 collective-permute-start.3
  17.5 1.5 copy-start.3
  17.5 1.5 collective-permute-start.1
  18.4 0.7 copy-start.4
  18.7 0.7 copy-start.5
  19.0 0.7 copy-start.6
  163.2 27.3 %all-to-all-start = ((f32[32,2,3,8,128]{4,3,2,1,0:T(8,128)}), f32[32,2,3,8,128]{4,3,2,1,0:T(8,128)S(1)}, u32[]{:S(2)}, u32[]{:S(2)}) async-start(f32[32,2,3,8,128]{4,3,2,1,0:T(8,128)} %bitcast.27), calls=%async_computation | async-start | bytes 1572864 | tf_op jit(solution)/shard_map/all_to_all | solution.py:484
  190.5 42.2 %copy-start = (f32[32,2,3,8,128]{4,3,2,1,0:T(8,128)}, f32[32,2,3,8,128]{4,3,2,1,0:T(8,128)S(1)}, u32[]{:S(2)}) copy-start(f32[32,2,3,8,128]{4,3,2,1,0:T(8,128)S(1)} %all-to-all-done.power_ref) | copy-start | bytes 2359300

commit v3 on v2

--- a/solution.py
+++ b/solution.py
@@ -10,8 +10,8 @@
 F32 = jnp.float32
 BF16 = jnp.bfloat16
 VMEM_LIMIT = 56 * 1024 * 1024
-PANEL = 8
-BROADCAST_UP_TO = 6
+LEAST = 0.0095
+CLOSE = 1e-3
 
 
 def elimination_levels(count):
@@ -56,84 +56,54 @@
     return pltpu.roll(x, x.shape[1] // 2, 1)
 
 
-def invert_batch(mat_ref, members, orbits):
-    width = 2 * orbits
-    blocks = orbits // PANEL
-    lane = lax.broadcasted_iota(jnp.int32, (PANEL, width), 1)
-    sub = lax.broadcasted_iota(jnp.int32, (PANEL, width), 0)
-    pivots = (lane < PANEL) | ((lane >= orbits) & (lane < orbits + PANEL))
-
-    def panel(p, unused):
-        rows = pl.ds(pl.multiple_of(p * PANEL, PANEL), PANEL)
-        original = lax.rem(lane + p * PANEL, width)
-        sign = jnp.where(original < orbits, -1.0, 1.0).astype(F32)
-        tops = []
-        for m in members:
-            tops.append(mat_ref[m, rows, :])
-        hats = []
-        if len(members) > BROADCAST_UP_TO:
-            for k in range(PANEL):
-                here = sub == k
-                at_pivot = (lane == k) | (lane == orbits + k)
-                unit = jnp.where(here & (lane == k), 1.0, 0.0).astype(F32)
-                for n in range(len(tops)):
-                    r = tops[n]
-                    cr = jnp.broadcast_to(r[:, k : k + 1], r.shape)
-                    ci = jnp.broadcast_to(r[:, orbits + k : orbits + k + 1], r.shape)
-                    inv = 1.0 / cr[k : k + 1, :]
-                    r0 = jnp.where(at_pivot, unit, r)
-                    row = r0[k : k + 1, :] * inv
-                    hat = half_roll(r0)[k : k + 1, :] * (sign[k : k + 1, :] * inv)
-                    tops[n] = jnp.where(here, row, r0 - cr * row - ci * hat)
-            for r in tops:
-                hats.append(half_roll(r) * sign)
-        else:
-            eye = jnp.where(lane == sub, 1.0, 0.0).astype(F32)
-            turned = jnp.where(lane == sub + orbits, 1.0, 0.0).astype(F32) * sign
-            cols = []
-            for n in range(len(tops)):
-                r = tops[n]
-                cols.append(
-                    [
-                        (
-                            jnp.broadcast_to(r[:, j : j + 1], r.shape),
-                            jnp.broadcast_to(r[:, orbits + j : orbits + j + 1], r.shape),
-                        )
-                        for j in range(PANEL)
-                    ]
-                )
-                hats.append(jnp.where(pivots, turned, half_roll(r) * sign))
-                tops[n] = jnp.where(pivots, eye, r)
-            for k in range(PANEL):
-                here = sub == k
-                for n in range(len(tops)):
-                    r, hat = tops[n], hats[n]
-                    cr, ci = cols[n][k]
-                    inv = 1.0 / cr[k : k + 1, :]
-                    ur, ui = cr * inv, ci * inv
-                    for j in range(k + 1, PANEL):
-                        er, ei = cols[n][j]
-                        fr, fi = er[k : k + 1, :], ei[k : k + 1, :]
-                        cols[n][j] = (
-                            jnp.where(here, fr * inv, er - ur * fr + ui * fi),
-                            jnp.where(here, fi * inv, ei - ur * fi - ui * fr),
-                        )
-                    row, hat_row = r[k : k + 1, :], hat[k : k + 1, :]
-                    tops[n] = jnp.where(here, row * inv, r - ur * row - ui * hat_row)
-                    hats[n] = jnp.where(here, hat_row * inv, hat - ur * hat_row + ui * row)
-        for n, m in enumerate(members):
-            r, hat = tops[n], hats[n]
-            for i in range(blocks):
-                block = mat_ref[m, PANEL * i : PANEL * (i + 1), :]
-                out = jnp.where(pivots, 0.0, block)
-                for j in range(PANEL):
-                    out = out - jnp.broadcast_to(block[:, j : j + 1], out.shape) * r[j : j + 1, :]
-                    out = out - jnp.broadcast_to(block[:, orbits + j : orbits + j + 1], out.shape) * hat[j : j + 1, :]
-                mat_ref[m, PANEL * i : PANEL * (i + 1), :] = pltpu.roll(out, width - PANEL, 1)
-            mat_ref[m, rows, :] = pltpu.roll(r, width - PANEL, 1)
-        return 0
-
-    lax.fori_loop(0, blocks, panel, 0)
+def turn_rows(z):
+    low = lax.broadcasted_iota(jnp.int32, z.shape, 1) < z.shape[1] // 2
+    turned = half_roll(z)
+    return jnp.concatenate([z, jnp.where(low, -turned, turned)], axis=0)
+
+
+def packed_mm(a, b):
+    full = turn_rows(b)
+    a1 = a.astype(BF16)
+    a2 = (a - a1.astype(F32)).astype(BF16)
+    b1 = full.astype(BF16)
+    b2 = (full - b1.astype(F32)).astype(BF16)
+    left = jnp.concatenate([a1, a2, a1], axis=1)
+    right = jnp.concatenate([b1, b1, b2], axis=0)
+    return lax.dot_general(left, right, (((1,), (0,)), ((), ())), preferred_element_type=F32)
+
+
+def invert_batch(mat_ref, inv_ref, members, top):
+    shape = mat_ref.shape[1:]
+    lane = lax.broadcasted_iota(jnp.int32, shape, 1)
+    sub = lax.broadcasted_iota(jnp.int32, shape, 0)
+    eye = jnp.where(lane == sub, 1.0, 0.0).astype(F32)
+    total = top + LEAST
+    for m in members:
+        inv_ref[m] = eye * (2.0 / total)
+
+    def body(reach):
+        squared = reach * reach
+        gain = 2.0 / (2.0 - squared)
+        after = squared * gain * 0.5
+        squared_after = after * after
+        gain_after = 2.0 / (2.0 - squared_after)
+        mats = [mat_ref[m] for m in members]
+        guesses = [inv_ref[m] for m in members]
+        closeness = [packed_mm(a, x) for a, x in zip(mats, guesses)]
+        pairs = [
+            packed_mm(jnp.concatenate([x, t], axis=0), (2.0 * eye - t) * gain) for x, t in zip(guesses, closeness)
+        ]
+        count = shape[0]
+        for m, pair in zip(members, pairs):
+            inv_ref[m] = packed_mm(pair[:count], (2.0 * eye - pair[count:]) * gain_after)
+        return squared_after * gain_after * 0.5
+
+    lax.while_loop(lambda reach: reach > CLOSE, body, (top - LEAST) / total)
+    guesses = [inv_ref[m] for m in members]
+    rests = [eye - mm(mat_ref[m], turn_rows(x)) for m, x in zip(members, guesses)]
+    for m, x, rest in zip(members, guesses, rests):
+        inv_ref[m] = x + packed_mm(x, rest)
 
 
 def link_places(slabs, mine, levels):
@@ -170,7 +140,7 @@
     (slabs, mine, orbits, groups, energy_groups, per, orb_per) = plan
     pq_ref, src_ref, set_ref = refs[0], refs[1], refs[2]
     peers = refs[3 : 3 + 2 * (groups - 1)]
-    power_ref, inv, w1, w2, up1, dn1, up2, dn2, sol, gains, data, mat, rhs = refs[3 + 2 * (groups - 1) :]
+    power_ref, inv, w1, w2, up1, dn1, up2, dn2, sol, gains, data, mat, rhs, near = refs[3 + 2 * (groups - 1) :]
     width = 2 * orbits
     levels, root = elimination_levels(slabs)
     places, _ = link_places(slabs, mine, levels)
@@ -198,9 +168,6 @@
     def real_rows(z):
         return jnp.concatenate([jnp.where(low, z, -z), half_roll(z)], axis=0)
 
-    def trans_rows(z):
-        return jnp.concatenate([z, jnp.where(low, -half_roll(z), half_roll(z))], axis=0)
-
     def real_left(t):
         top, bottom = t[:orbits], t[orbits:]
         return jnp.concatenate(
@@ -225,24 +192,29 @@
     def factor_q(s):
         return data[s, orbits : 2 * orbits, :]
 
+    largest = None
     for s in range(slabs):
         zq = factor_q(s)
-        base = mm_nt(zq, trans_rows(zq))
+        base = mm_nt(zq, turn_rows(zq))
         if s + 1 < slabs:
             zp = factor_p(s + 1)
-            base = base + mm_nt(zp, trans_rows(zp))
+            base = base + mm_nt(zp, turn_rows(zp))
             rp = real_rows(zp)
             rq = real_rows(factor_q(s + 1))
             up1[s] = -mm_nt(rp, rq)
             dn1[s] = -mm_nt(rq, rp)
         if s == 0:
             zp = factor_p(0)
-            base = base + mm_nt(zp, trans_rows(zp))
+            base = base + mm_nt(zp, turn_rows(zp))
         for e in range(mine):
             settings = data[s, pl.ds(2 * width + first + e, 1), :]
             gains[s * mine + e] = settings
-            mat[s * mine + e] = base + jnp.where(diag_lane, settings, 0.0)
+            block = base + jnp.where(diag_lane, settings, 0.0)
+            mat[s * mine + e] = block
             rhs[s * mine + e] = data[s, width : 2 * width, :]
+            sums = jnp.sum(jnp.abs(block), axis=0, keepdims=True)
+            largest = sums if largest is None else jnp.maximum(largest, sums)
+    top = 1.01 * jnp.max(largest + half_roll(largest))
 
     def held(key):
         basic, place = places[key]
@@ -262,11 +234,11 @@
         return jnp.where(low_all, to_left, to_right)
 
     for depth, level in enumerate(levels):
-        invert_batch(mat, [node * mine + e for node, _, _ in level for e in range(mine)], orbits)
+        invert_batch(mat, near, [node * mine + e for node, _, _ in level for e in range(mine)], top)
         for node, left, right in level:
             for e in range(mine):
                 m = node * mine + e
-                full = real_rows(half_roll(mat[m]))
+                full = real_rows(near[m])
                 inv[m] = full
                 stacked = jnp.concatenate([couplings(depth, node, left, right, e), rhs[m]], axis=1)
                 step = mm(full, stacked)
@@ -292,10 +264,10 @@
                     if left is not None:
                         _, downs, place = held((depth + 1, left, right, e))
                         downs[place] = -real_left(change[:, :width])
-    invert_batch(mat, [root * mine + e for e in range(mine)], orbits)
+    invert_batch(mat, near, [root * mine + e for e in range(mine)], top)
     for e in range(mine):
         m = root * mine + e
-        full = real_rows(half_roll(mat[m]))
+        full = real_rows(near[m])
         inv[m] = full
         sol[m] = mm(full, rhs[m])
     climb(levels, mine, w1, w2, sol)
@@ -382,6 +354,7 @@
             pltpu.VMEM((slabs, 2 * width + local, columns), F32),
             pltpu.VMEM((nodes, orbits, width), F32),
             pltpu.VMEM((nodes, width, columns), F32),
+            pltpu.VMEM((nodes, orbits, width), F32),
         ],
         compiler_params=pltpu.CompilerParams(vmem_limit_bytes=VMEM_LIMIT),
         name="solve_retarded",

time: 240 us -> 128 us (0.53)
  Pallas kernels: 164 us -> 51.6 us
    pallas_call x1, Pallas kernels: 144 us -> 30.7 us  [solve_retarded(): pl.pallas_call(functools.partial(retarded_kernel, plan), out_shape=[jax.S...]
  transfers between devices with their start and end apart: 7 -> 7, of which waited for: 6 -> 6; matrix products, arithmetic and copies ran while one was open for 0% -> 1% of each run, Pallas kernels for 6% -> 11%
where the time goes in v3:
time: 128 us; the launch traced here: 127 us
  Pallas kernels  51.6 us (40%)
  blocking collectives  42.2 us (33%)
  waiting for transfers between devices  18.1 us (14%)
  starting transfers between devices  10.2 us (8%)
  other arithmetic  3.2 us (2%)
  local copies, waits for them, and re-layouts  1.76 us (1%)
    all_to_all x1, blocking collectives, spread(): lax.all_to_all(array, ('slab', 'energy'), split_axis=0, concat_axis=0, ti...  42.2 us
    pallas_call x1, Pallas kernels, solve_retarded(): pl.pallas_call(functools.partial(retarded_kernel, plan), out_shape=[jax.S...  30.7 us
    pallas_call x1, Pallas kernels, solve_lesser(): pl.pallas_call(functools.partial(lesser_kernel, plan), out_shape=jax.Shap...  13.8 us
    ppermute x3, waiting for transfers between devices, per_device(): lax.ppermute(parcel, 'slab', [(g, g ^ k) for g in range(groups)])  9.27 us
    all_to_all x1, waiting for transfers between devices, spread(): lax.all_to_all(array, ('slab', 'energy'), split_axis=0, concat_axis=0, ti...  8.21 us
    pallas_call x1, Pallas kernels, correlate(): pl.pallas_call(functools.partial(correlate_kernel, order), grid=(per,), o...  7.08 us
    all_to_all x1, starting transfers between devices, spread(): lax.all_to_all(array, ('slab', 'energy'), split_axis=0, concat_axis=0, ti...  5.35 us
    ppermute x3, starting transfers between devices, per_device(): lax.ppermute(parcel, 'slab', [(g, g ^ k) for g in range(groups)])  4.6 us
  transfers between devices with their start and end apart: 7, of which 6 were waited for; matrix products, arithmetic and copies ran while one was open for 1% of the time, Pallas kernels for 11%

profile of v3, /device:TPU:0, one launch (start us, length us, event | category | flops | bytes accessed | tf_op | source)
XLA Modules:
  0.0 127.1 jit_solution(7054002670952762344)
XLA Ops:
  0.0 0.8 maximum_bitcast_fusion.refs_2_
  0.8 0.0 copy-start.7
  0.8 1.1 slice_bitcast_fusion.1
  1.9 1.7 %broadcast_select_fusion = (f32[3,128,128]{2,1,0:T(8,128)S(1)}, f32[3,128,128]{2,1,0:T(8,128)}) fusion(pred[]{:T(512)S(6)} %eq.5, f32[3,2,64,128]{3,2,1,0:T(8,128)} %param.9, f32[3,64,64]{2,1,0:T(8,128)S(1)} %get-tuple-element.30, f32[3,64,64]{2,1,0:T(8,128)S(1)} %get-tuple-element.29, f32[3,64,64]{2,1,0:T(8,128)S(1)} %get-tuple-element.31, ...), kind=kLoop, calls=%fused_computation.6 | loop fusion | flops 196608 | bytes 786433 | tf_op jit(solution)/shard_map/jit(_where)/select_n | solution.py:444
  3.6 4.0 %collective-permute-start.4 = (f32[3,136,128]{2,1,0:T(8,128)S(1)}, f32[3,136,128]{2,1,0:T(8,128)S(1)}, u32[]{:S(2)}, u32[]{:S(2)}) collective-permute-start(f32[3,136,128]{2,1,0:T(8,128)S(1)} %pad_maximum_fusion), channel_id=1, source_target_pairs={{0,24},{8,16},{16,8},{24,0},{1,25},{9,17},{17,9},{25,1},{2,26},{10... | collective-permute-start | bytes 626696 | tf_op jit(solution)/shard_map/ppermute | solution.py:447
  7.6 0.5 collective-permute-start.2
  8.1 0.1 collective-permute-start
  8.2 5.4 %collective-permute-done.4.refs_7_ = f32[3,136,128]{2,1,0:T(8,128)S(1)} collective-permute-done((f32[3,136,128]{2,1,0:T(8,128)S(1)}, f32[3,136,128]{2,1,0:T(8,128)S(1)}, u32[]{:S(2)}, u32[]{:S(2)}) %collective-permute-start.4) | collective-permute-done | bytes 208928 | tf_op jit(solution)/shard_map/ppermute | solution.py:447
  13.6 0.0 copy-start.1
  13.6 0.0 collective-permute-start.5
  13.6 3.6 %collective-permute-done.2.refs_5_ = f32[3,136,128]{2,1,0:T(8,128)S(1)} collective-permute-done((f32[3,136,128]{2,1,0:T(8,128)S(1)}, f32[3,136,128]{2,1,0:T(8,128)S(1)}, u32[]{:S(2)}, u32[]{:S(2)}) %collective-permute-start.2) | collective-permute-done | bytes 208928 | tf_op jit(solution)/shard_map/ppermute | solution.py:447
  17.2 0.0 collective-permute-start.3
  17.2 0.3 collective-permute-done.refs_3_
  17.5 0.2 collective-permute-start.1
  17.7 0.7 pad_add_fusion.where_ref
  18.4 0.0 collective-permute-done.5.refs_8_
  18.4 0.3 collective-permute-done.3.refs_6_
  18.7 0.3 collective-permute-done.1.refs_4_
  19.0 0.0 copy-done.7
  19.0 0.0 copy-done.1
  19.0 0.0 copy-done.2
  19.0 0.0 copy-done.3
  19.0 0.1 copy-done.4
  19.1 0.3 copy-done.5
  19.4 0.3 copy-done.6
  19.7 30.7 %solve_retarded.1 = (f32[4,8,2,3,8,128]{5,4,3,2,1,0:T(8,128)}, f32[24,128,128]{2,1,0:T(8,128)}, f32[24,128,128]{2,1,0:T(8,128)}, f32[24,128,128]{2,1,0:T(8,128)}...) custom-call(s32[3]{0:T(128)} %pad_add_fusion.where_ref, ...), custom_call_target="tpu_custom_call" | custom-call | tf_op jit(solution)/shard_map/solve_retarded/pallas_call | solution.py:348
  50.4 5.4 %all-to-all-start = ((f32[32,2,3,8,128]{4,3,2,1,0:T(8,128)}), f32[32,2,3,8,128]{4,3,2,1,0:T(8,128)S(1)}, u32[]{:S(2)}, u32[]{:S(2)}) async-start(f32[32,2,3,8,128]{4,3,2,1,0:T(8,128)} %bitcast.27), calls=%async_computation | async-start | bytes 1572864 | tf_op jit(solution)/shard_map/all_to_all | solution.py:457
  55.8 13.8 %solve_lesser.1 = f32[4,8,2,2,3,8,128]{6,5,4,3,2,1,0:T(8,128)} custom-call(f32[24,128,128]{2,1,0:T(8,128)} %get-tuple-element.16.inv, f32[24,128,128]{2,1,0:T(8,128)} %get-tuple-element.17.w1, f32[24,128,128]{2,1,0:T(8,128)} %get-tuple-element.18.w2, f32[11,128,128]{2,1,0:T(8,128)} %get-tuple-element.19.up1, f32[11,128,128]{2,1,0:T(8,128)} %get-tuple-element.20.dn1, ...), custom_call_target="tpu_custom_call" | custom-call | tf_op jit(solution)/shard_map/solve_lesser/pallas_call | solution.py:367
  69.5 8.2 %all-to-all-done.power_ref = f32[32,2,3,8,128]{4,3,2,1,0:T(8,128)S(1)} async-done(((f32[32,2,3,8,128]{4,3,2,1,0:T(8,128)}), f32[32,2,3,8,128]{4,3,2,1,0:T(8,128)S(1)}, u32[]{:S(2)}, u32[]{:S(2)}) %all-to-all-start) | async-done | bytes 786464 | tf_op jit(solution)/shard_map/all_to_all | solution.py:457
  77.7 42.2 %all_to_all.10.got_ref = f32[32,2,2,3,8,128]{5,4,3,2,1,0:T(8,128)} all-to-all(f32[32,2,2,3,8,128]{5,4,3,2,1,0:T(8,128)} %bitcast.25), channel_id=1, replica_groups=mesh['slab'=4,'energy'=8] {'slab','energy'}, dimensions={0} | all-to-all | bytes 3145728 | tf_op jit(solution)/shard_map/all_to_all | solution.py:457
  120.0 0.0 copy-done
  120.0 7.1 %correlate.1 = f32[2,64,3,8,128]{4,3,2,1,0:T(8,128)} custom-call(f32[32,2,3,8,128]{4,3,2,1,0:T(8,128)} %copy-done, f32[32,2,2,3,8,128]{5,4,3,2,1,0:T(8,128)} %all_to_all.10.got_ref), custom_call_target="tpu_custom_call" | custom-call | tf_op jit(solution)/shard_map/correlate/pallas_call | solution.py:409
  (7 shorter events, 0.0 us)
Async XLA Ops:
  0.8 18.2 %copy-start.7 = (f32[3,8,128]{2,1,0:T(8,128)}, f32[3,8,128]{2,1,0:T(8,128)S(1)}, u32[]{:S(2)}) copy-start(f32[3,8,128]{2,1,0:T(8,128)S(1)} %maximum_bitcast_fusion.refs_2_) | copy-start | bytes 36868
  3.6 10.0 %collective-permute-start.4 = (f32[3,136,128]{2,1,0:T(8,128)S(1)}, f32[3,136,128]{2,1,0:T(8,128)S(1)}, u32[]{:S(2)}, u32[]{:S(2)}) collective-permute-start(f32[3,136,128]{2,1,0:T(8,128)S(1)} %pad_maximum_fusion), channel_id=1, source_target_pairs={{0,24},{8,16},{16,8},{24,0},{1,25},{9,17},{17,9},{25,1},{2,26},{10... | collective-permute-start | bytes 626696 | tf_op jit(solution)/shard_map/ppermute | solution.py:447
  7.6 9.6 %collective-permute-start.2 = (f32[3,136,128]{2,1,0:T(8,128)S(1)}, f32[3,136,128]{2,1,0:T(8,128)S(1)}, u32[]{:S(2)}, u32[]{:S(2)}) collective-permute-start(f32[3,136,128]{2,1,0:T(8,128)S(1)} %pad_maximum_fusion), channel_id=1, source_target_pairs={{0,16},{8,24},{16,0},{24,8},{1,17},{9,25},{17,1},{25,9},{2,18},{10... | collective-permute-start | bytes 626696 | tf_op jit(solution)/shard_map/ppermute | solution.py:447
  8.1 9.4 %collective-permute-start = (f32[3,136,128]{2,1,0:T(8,128)S(1)}, f32[3,136,128]{2,1,0:T(8,128)S(1)}, u32[]{:S(2)}, u32[]{:S(2)}) collective-permute-start(f32[3,136,128]{2,1,0:T(8,128)S(1)} %pad_maximum_fusion), channel_id=1, source_target_pairs={{0,8},{8,0},{16,24},{24,16},{1,9},{9,1},{17,25},{25,17},{2,10},{10... | collective-permute-start | bytes 626696 | tf_op jit(solution)/shard_map/ppermute | solution.py:447
  13.6 5.4 %copy-start.1 = (f32[3,136,128]{2,1,0:T(8,128)}, f32[3,136,128]{2,1,0:T(8,128)S(1)}, u32[]{:S(2)}) copy-start(f32[3,136,128]{2,1,0:T(8,128)S(1)} %collective-permute-done.4.refs_7_) | copy-start | bytes 626692
  13.6 4.8 %collective-permute-start.5 = (f32[3,136,128]{2,1,0:T(8,128)S(1)}, f32[3,136,128]{2,1,0:T(8,128)S(1)}, u32[]{:S(2)}, u32[]{:S(2)}) collective-permute-start(f32[3,136,128]{2,1,0:T(8,128)S(1)} %collective-permute-done.4.refs_7_), channel_id=1, source_target_pairs={{0,1},{1,0},{2,3},{3,2},{4,5},{5,4},{6,7},{7,6},{8,9},{9,8},{10,11... | collective-permute-start | bytes 626696 | tf_op jit(solution)/shard_map/ppermute | solution.py:450
  17.2 1.8 %copy-start.2 = (f32[3,136,128]{2,1,0:T(8,128)}, f32[3,136,128]{2,1,0:T(8,128)S(1)}, u32[]{:S(2)}) copy-start(f32[3,136,128]{2,1,0:T(8,128)S(1)} %collective-permute-done.2.refs_5_) | copy-start | bytes 626692
  17.2 1.5 %collective-permute-start.3 = (f32[3,136,128]{2,1,0:T(8,128)S(1)}, f32[3,136,128]{2,1,0:T(8,128)S(1)}, u32[]{:S(2)}, u32[]{:S(2)}) collective-permute-start(f32[3,136,128]{2,1,0:T(8,128)S(1)} %collective-permute-done.2.refs_5_), channel_id=1, source_target_pairs={{0,1},{1,0},{2,3},{3,2},{4,5},{5,4},{6,7},{7,6},{8,9},{9,8},{10,11... | collective-permute-start | bytes 626696 | tf_op jit(solution)/shard_map/ppermute | solution.py:450
  17.5 1.5 %copy-start.3 = (f32[3,136,128]{2,1,0:T(8,128)}, f32[3,136,128]{2,1,0:T(8,128)S(1)}, u32[]{:S(2)}) copy-start(f32[3,136,128]{2,1,0:T(8,128)S(1)} %collective-permute-done.refs_3_) | copy-start | bytes 626692
  17.5 1.5 %collective-permute-start.1 = (f32[3,136,128]{2,1,0:T(8,128)S(1)}, f32[3,136,128]{2,1,0:T(8,128)S(1)}, u32[]{:S(2)}, u32[]{:S(2)}) collective-permute-start(f32[3,136,128]{2,1,0:T(8,128)S(1)} %collective-permute-done.refs_3_), channel_id=1, source_target_pairs={{0,1},{1,0},{2,3},{3,2},{4,5},{5,4},{6,7},{7,6},{8,9},{9,8},{10,11... | collective-permute-start | bytes 626696 | tf_op jit(solution)/shard_map/ppermute | solution.py:450
  18.4 0.7 copy-start.4
  18.7 0.7 copy-start.5
  19.0 0.7 copy-start.6
  50.4 27.3 %all-to-all-start = ((f32[32,2,3,8,128]{4,3,2,1,0:T(8,128)}), f32[32,2,3,8,128]{4,3,2,1,0:T(8,128)S(1)}, u32[]{:S(2)}, u32[]{:S(2)}) async-start(f32[32,2,3,8,128]{4,3,2,1,0:T(8,128)} %bitcast.27), calls=%async_computation | async-start | bytes 1572864 | tf_op jit(solution)/shard_map/all_to_all | solution.py:457
  77.7 42.2 %copy-start = (f32[32,2,3,8,128]{4,3,2,1,0:T(8,128)}, f32[32,2,3,8,128]{4,3,2,1,0:T(8,128)S(1)}, u32[]{:S(2)}) copy-start(f32[32,2,3,8,128]{4,3,2,1,0:T(8,128)S(1)} %all-to-all-done.power_ref) | copy-start | bytes 2359300

commit v4 on v3

--- a/solution.py
+++ b/solution.py
@@ -10,8 +10,10 @@
 F32 = jnp.float32
 BF16 = jnp.bfloat16
 VMEM_LIMIT = 56 * 1024 * 1024
+SMALL_LIMIT = 16 * 1024 * 1024
 LEAST = 0.0095
 CLOSE = 1e-3
+STRIDE = 4
 
 
 def elimination_levels(count):
@@ -44,6 +46,16 @@
     return lax.dot_general(left, right, (((1,), (0,)), ((), ())), preferred_element_type=F32)
 
 
+def mm_three(a, b):
+    a1 = a.astype(BF16)
+    a2 = (a - a1.astype(F32)).astype(BF16)
+    b1 = b.astype(BF16)
+    b2 = (b - b1.astype(F32)).astype(BF16)
+    left = jnp.concatenate([a1, a2, a1], axis=1)
+    right = jnp.concatenate([b1, b1, b2], axis=0)
+    return lax.dot_general(left, right, (((1,), (0,)), ((), ())), preferred_element_type=F32)
+
+
 def mm_nt(a, b):
     a1, a2, a3 = thirds(a)
     b1, b2, b3 = thirds(b)
@@ -63,47 +75,60 @@
 
 
 def packed_mm(a, b):
-    full = turn_rows(b)
-    a1 = a.astype(BF16)
-    a2 = (a - a1.astype(F32)).astype(BF16)
-    b1 = full.astype(BF16)
-    b2 = (full - b1.astype(F32)).astype(BF16)
-    left = jnp.concatenate([a1, a2, a1], axis=1)
-    right = jnp.concatenate([b1, b1, b2], axis=0)
-    return lax.dot_general(left, right, (((1,), (0,)), ((), ())), preferred_element_type=F32)
+    return mm_three(a, turn_rows(b))
 
 
 def invert_batch(mat_ref, inv_ref, members, top):
     shape = mat_ref.shape[1:]
+    count = shape[0]
     lane = lax.broadcasted_iota(jnp.int32, shape, 1)
     sub = lax.broadcasted_iota(jnp.int32, shape, 0)
     eye = jnp.where(lane == sub, 1.0, 0.0).astype(F32)
     total = top + LEAST
-    for m in members:
-        inv_ref[m] = eye * (2.0 / total)
-
-    def body(reach):
+
+    def factor_of(reach):
         squared = reach * reach
         gain = 2.0 / (2.0 - squared)
-        after = squared * gain * 0.5
-        squared_after = after * after
-        gain_after = 2.0 / (2.0 - squared_after)
-        mats = [mat_ref[m] for m in members]
-        guesses = [inv_ref[m] for m in members]
-        closeness = [packed_mm(a, x) for a, x in zip(mats, guesses)]
-        pairs = [
-            packed_mm(jnp.concatenate([x, t], axis=0), (2.0 * eye - t) * gain) for x, t in zip(guesses, closeness)
-        ]
-        count = shape[0]
-        for m, pair in zip(members, pairs):
-            inv_ref[m] = packed_mm(pair[:count], (2.0 * eye - pair[count:]) * gain_after)
-        return squared_after * gain_after * 0.5
-
-    lax.while_loop(lambda reach: reach > CLOSE, body, (top - LEAST) / total)
-    guesses = [inv_ref[m] for m in members]
-    rests = [eye - mm(mat_ref[m], turn_rows(x)) for m, x in zip(members, guesses)]
-    for m, x, rest in zip(members, guesses, rests):
+        return gain, 0.5 * squared * gain
+
+    def steps(xs, ts, reach, number):
+        for step in range(number):
+            gain, reach = factor_of(reach)
+            bases = [(2.0 * eye - t) * gain for t in ts]
+            if step + 1 < number:
+                pairs = [packed_mm(jnp.concatenate([x, t], axis=0), base) for x, t, base in zip(xs, ts, bases)]
+                xs = [pair[:count] for pair in pairs]
+                ts = [pair[count:] for pair in pairs]
+            else:
+                xs = [packed_mm(x, base) for x, base in zip(xs, bases)]
+        for m, x in zip(members, xs):
+            inv_ref[m] = x
+        return reach
+
+    reach = (top - LEAST) / total
+    start = 2.0 / total
+    gain, reach = factor_of(reach)
+    ts = [mat_ref[m] * start for m in members]
+    bases = [(2.0 * eye - t) * gain for t in ts]
+    xs = [base * start for base in bases]
+    ts = [packed_mm(t, base) for t, base in zip(ts, bases)]
+    reach = steps(xs, ts, reach, STRIDE - 1)
+
+    def body(reach):
+        xs = [inv_ref[m] for m in members]
+        ts = [packed_mm(mat_ref[m], x) for m, x in zip(members, xs)]
+        return steps(xs, ts, reach, STRIDE)
+
+    lax.while_loop(lambda reach: reach > CLOSE, body, reach)
+    xs = [inv_ref[m] for m in members]
+    rests = [eye - mm(mat_ref[m], turn_rows(x)) for m, x in zip(members, xs)]
+    for m, x, rest in zip(members, xs, rests):
         inv_ref[m] = x + packed_mm(x, rest)
+
+
+def slots(levels, root):
+    order = [node for level in levels for node, _, _ in level] + [root]
+    return {node: place for place, node in enumerate(order)}
 
 
 def link_places(slabs, mine, levels):
@@ -121,28 +146,41 @@
     return places, spare
 
 
-def climb(levels, mine, w1, w2, sol):
+def climb(levels, spot, mine, w1, w2, sol, finished):
     for level in reversed(levels):
         for node, left, right in level:
             for e in range(mine):
-                m = node * mine + e
+                m = spot[node] * mine + e
                 if left is not None and right is not None:
                     both = jnp.concatenate([w1[m], w2[m]], axis=1)
-                    sides = jnp.concatenate([sol[left * mine + e], sol[right * mine + e]], axis=0)
-                    sol[m] = sol[m] - mm(both, sides)
+                    sides = jnp.concatenate([sol[spot[left] * mine + e], sol[spot[right] * mine + e]], axis=0)
+                    sol[m] = sol[m] - mm_three(both, sides)
                 elif left is not None:
-                    sol[m] = sol[m] - mm(w1[m], sol[left * mine + e])
+                    sol[m] = sol[m] - mm_three(w1[m], sol[spot[left] * mine + e])
                 elif right is not None:
-                    sol[m] = sol[m] - mm(w2[m], sol[right * mine + e])
+                    sol[m] = sol[m] - mm_three(w2[m], sol[spot[right] * mine + e])
+        finished([node for node, _, _ in level])
 
 
 def retarded_kernel(plan, where_ref, *refs):
     (slabs, mine, orbits, groups, energy_groups, per, orb_per) = plan
     pq_ref, src_ref, set_ref = refs[0], refs[1], refs[2]
     peers = refs[3 : 3 + 2 * (groups - 1)]
-    power_ref, inv, w1, w2, up1, dn1, up2, dn2, sol, gains, data, mat, rhs, near = refs[3 + 2 * (groups - 1) :]
+    power_ref, gains = refs[3 + 2 * (groups - 1) : 5 + 2 * (groups - 1)]
+    outs = refs[5 + 2 * (groups - 1) : 13 + 2 * (groups - 1)]
+    inv, w1, w2, up1, dn1, up2, dn2, sol, data, mat, rhs, near, sems = refs[13 + 2 * (groups - 1) :]
+    stores = (inv, w1, w2, up1, dn1, up2, dn2, sol)
+    copies = []
+
+    def copy_out(which, low_place, high_place):
+        part = pl.ds(low_place, high_place - low_place)
+        copy = pltpu.make_async_copy(stores[which].at[part], outs[which].at[part], sems.at[len(copies)])
+        copy.start()
+        copies.append(copy)
+
     width = 2 * orbits
     levels, root = elimination_levels(slabs)
+    spot = slots(levels, root)
     places, _ = link_places(slabs, mine, levels)
     lane = lax.broadcasted_iota(jnp.int32, (orbits, width), 1)
     sub = lax.broadcasted_iota(jnp.int32, (orbits, width), 0)
@@ -186,35 +224,36 @@
     def packed_right(t):
         return jnp.where(low, half_roll(t[:orbits]), t[orbits:])
 
-    def factor_p(s):
-        return data[s, 0:orbits, :]
-
-    def factor_q(s):
-        return data[s, orbits : 2 * orbits, :]
-
     largest = None
+    pps, qqs = [], []
     for s in range(slabs):
-        zq = factor_q(s)
-        base = mm_nt(zq, turn_rows(zq))
+        both = data[s, 0:width, :]
+        zp, zq = both[:orbits], both[orbits:]
+        with_p = mm_nt(both, turn_rows(zp))
+        with_q = mm_nt(both, turn_rows(zq))
+        pps.append(with_p[:orbits])
+        qqs.append(with_q[orbits:])
+        if s > 0:
+            up1[s - 1] = -real_rows(with_q[:orbits])
+            dn1[s - 1] = -real_rows(with_p[orbits:])
+    for s in range(slabs):
+        base = qqs[s]
         if s + 1 < slabs:
-            zp = factor_p(s + 1)
-            base = base + mm_nt(zp, turn_rows(zp))
-            rp = real_rows(zp)
-            rq = real_rows(factor_q(s + 1))
-            up1[s] = -mm_nt(rp, rq)
-            dn1[s] = -mm_nt(rq, rp)
+            base = base + pps[s + 1]
         if s == 0:
-            zp = factor_p(0)
-            base = base + mm_nt(zp, turn_rows(zp))
+            base = base + pps[0]
         for e in range(mine):
             settings = data[s, pl.ds(2 * width + first + e, 1), :]
-            gains[s * mine + e] = settings
+            m = spot[s] * mine + e
+            gains[m] = settings
             block = base + jnp.where(diag_lane, settings, 0.0)
-            mat[s * mine + e] = block
-            rhs[s * mine + e] = data[s, width : 2 * width, :]
+            mat[m] = block
+            rhs[m] = data[s, width : 2 * width, :]
             sums = jnp.sum(jnp.abs(block), axis=0, keepdims=True)
             largest = sums if largest is None else jnp.maximum(largest, sums)
     top = 1.01 * jnp.max(largest + half_roll(largest))
+    copy_out(3, 0, slabs - 1)
+    copy_out(4, 0, slabs - 1)
 
     def held(key):
         basic, place = places[key]
@@ -234,56 +273,74 @@
         return jnp.where(low_all, to_left, to_right)
 
     for depth, level in enumerate(levels):
-        invert_batch(mat, near, [node * mine + e for node, _, _ in level for e in range(mine)], top)
+        invert_batch(mat, near, [spot[node] * mine + e for node, _, _ in level for e in range(mine)], top)
         for node, left, right in level:
             for e in range(mine):
-                m = node * mine + e
+                m = spot[node] * mine + e
                 full = real_rows(near[m])
                 inv[m] = full
                 stacked = jnp.concatenate([couplings(depth, node, left, right, e), rhs[m]], axis=1)
                 step = mm(full, stacked)
                 links_step, rhs_step = step[:, :width], step[:, width:]
                 sol[m] = rhs_step
+                sides = []
                 if left is not None:
                     w1[m] = real_left(links_step)
                     ups, _, place = held((depth, left, node, e))
-                    change = mm(ups[place], step)
-                    ml = left * mine + e
-                    mat[ml] = mat[ml] - packed_left(change[:, :width])
-                    rhs[ml] = rhs[ml] - change[:, width:]
-                    if right is not None:
-                        ups, _, place = held((depth + 1, left, right, e))
-                        ups[place] = -real_right(change[:, :width])
+                    sides.append(ups[place])
                 if right is not None:
                     w2[m] = real_right(links_step)
                     _, downs, place = held((depth, node, right, e))
-                    change = mm(downs[place], step)
-                    mr = right * mine + e
-                    mat[mr] = mat[mr] - packed_right(change[:, :width])
-                    rhs[mr] = rhs[mr] - change[:, width:]
-                    if left is not None:
-                        _, downs, place = held((depth + 1, left, right, e))
-                        downs[place] = -real_left(change[:, :width])
-    invert_batch(mat, near, [root * mine + e for e in range(mine)], top)
+                    sides.append(downs[place])
+                change = mm(sides[0] if len(sides) == 1 else jnp.concatenate(sides, axis=0), step)
+                if left is not None:
+                    ml = spot[left] * mine + e
+                    mat[ml] = mat[ml] - packed_left(change[:width, :width])
+                    rhs[ml] = rhs[ml] - change[:width, width:]
+                if right is not None:
+                    mr = spot[right] * mine + e
+                    mat[mr] = mat[mr] - packed_right(change[-width:, :width])
+                    rhs[mr] = rhs[mr] - change[-width:, width:]
+                if left is not None and right is not None:
+                    ups, downs, place = held((depth + 1, left, right, e))
+                    ups[place] = -real_right(change[:width, :width])
+                    downs[place] = -real_left(change[-width:, :width])
+        span = [spot[node] * mine for node, _, _ in level]
+        for which in range(3):
+            copy_out(which, span[0], span[-1] + mine)
+        made = [places[(depth + 1, l, r, e)][1] for _, l, r in level if l is not None and r is not None for e in range(mine)]
+        if made:
+            copy_out(5, made[0], made[-1] + 1)
+            copy_out(6, made[0], made[-1] + 1)
+    invert_batch(mat, near, [spot[root] * mine + e for e in range(mine)], top)
     for e in range(mine):
-        m = root * mine + e
+        m = spot[root] * mine + e
         full = real_rows(near[m])
         inv[m] = full
         sol[m] = mm(full, rhs[m])
-    climb(levels, mine, w1, w2, sol)
-    for s in range(slabs):
-        for e in range(mine):
-            x = sol[s * mine + e]
-            xr, xi = x[:orbits], x[orbits:]
-            power = xr * xr + xi * xi
-            for j in range(energy_groups):
-                power_ref[s // per, j, e, s % per, :, :] = power[j * orb_per : (j + 1) * orb_per, :]
-
-
-def lesser_kernel(plan, inv, w1, w2, up1, dn1, up2, dn2, ret, gains, out_ref, rhs, sol):
+    copy_out(0, spot[root] * mine, (spot[root] + 1) * mine)
+
+    def finished(nodes):
+        copy_out(7, spot[nodes[0]] * mine, (spot[nodes[-1]] + 1) * mine)
+        for s in nodes:
+            for e in range(mine):
+                x = sol[spot[s] * mine + e]
+                xr, xi = x[:orbits], x[orbits:]
+                power = xr * xr + xi * xi
+                for j in range(energy_groups):
+                    power_ref[s // per, j, e, s % per, :, :] = power[j * orb_per : (j + 1) * orb_per, :]
+
+    finished([root])
+    climb(levels, spot, mine, w1, w2, sol, finished)
+    for copy in copies:
+        copy.wait()
+
+
+def lesser_kernel(plan, gains, inv, w1, w2, up1, dn1, up2, dn2, ret, out_ref, rhs, sol):
     (slabs, mine, orbits, groups, energy_groups, per, orb_per) = plan
     width = 2 * orbits
     levels, root = elimination_levels(slabs)
+    spot = slots(levels, root)
     places, _ = link_places(slabs, mine, levels)
     lane = lax.broadcasted_iota(jnp.int32, (orbits, width), 1)
     sub = lax.broadcasted_iota(jnp.int32, (orbits, width), 0)
@@ -294,24 +351,30 @@
     for depth, level in enumerate(levels):
         for node, left, right in level:
             for e in range(mine):
-                m = node * mine + e
+                m = spot[node] * mine + e
                 step = mm(inv[m], rhs[m])
                 sol[m] = step
+                sides = []
                 if left is not None:
                     basic, place = places[(depth, left, node, e)]
-                    ml = left * mine + e
-                    rhs[ml] = rhs[ml] - mm((up1 if basic else up2)[place], step)
+                    sides.append((up1 if basic else up2)[place])
                 if right is not None:
                     basic, place = places[(depth, node, right, e)]
-                    mr = right * mine + e
-                    rhs[mr] = rhs[mr] - mm((dn1 if basic else dn2)[place], step)
+                    sides.append((dn1 if basic else dn2)[place])
+                change = mm(sides[0] if len(sides) == 1 else jnp.concatenate(sides, axis=0), step)
+                if left is not None:
+                    ml = spot[left] * mine + e
+                    rhs[ml] = rhs[ml] - change[:width]
+                if right is not None:
+                    mr = spot[right] * mine + e
+                    rhs[mr] = rhs[mr] - change[-width:]
     for e in range(mine):
-        m = root * mine + e
+        m = spot[root] * mine + e
         sol[m] = mm(inv[m], rhs[m])
-    climb(levels, mine, w1, w2, sol)
+    climb(levels, spot, mine, w1, w2, sol, lambda nodes: None)
     for s in range(slabs):
         for e in range(mine):
-            m = s * mine + e
+            m = spot[s] * mine + e
             x, y = ret[m], sol[m]
             xr, xi, yr, yi = x[:orbits], x[orbits:], y[:orbits], y[orbits:]
             re = xr * yr + xi * yi
@@ -322,6 +385,48 @@
                 out_ref[s // per, j, 1, e, s % per, :, :] = im[rows, :]
 
 
+def pack_kernel(where_ref, p_ref, q_ref, src_ref, shift_ref, gain_ref, factors_ref, settings_ref, parcel_ref):
+    per, _, orbits, _ = p_ref.shape
+    width = 2 * orbits
+    local = shift_ref.shape[0]
+    core = where_ref[2]
+    for i in range(per):
+        rows = [
+            jnp.concatenate([shift_ref[e, i : i + 1, :], gain_ref[e, i : i + 1, :]], axis=1) for e in range(local)
+        ]
+        settings = jnp.concatenate(rows, axis=0)
+        settings_ref[i] = settings
+        parcel_ref[i, width : width + local, :] = settings
+        factors_ref[i, 0:orbits, :] = jnp.concatenate([p_ref[i, 0], p_ref[i, 1]], axis=1)
+        factors_ref[i, orbits:width, :] = jnp.concatenate([q_ref[i, 0], q_ref[i, 1]], axis=1)
+
+    @pl.when(core == 0)
+    def _():
+        parcel_ref[:, 0:width, :] = factors_ref[...]
+
+    @pl.when(core != 0)
+    def _():
+        for i in range(per):
+            parcel_ref[i, 0:orbits, :] = src_ref[i, 0]
+            parcel_ref[i, orbits:width, :] = src_ref[i, 1]
+
+
+def pack(where, link_p, link_q, sources, shift, lesser_gain):
+    per, _, orbits, _ = link_p.shape
+    width = 2 * orbits
+    columns = sources.shape[-1]
+    local = shift.shape[0]
+    shapes = [(per, width, width), (per, local, width), (per, width + local, columns)]
+    return pl.pallas_call(
+        pack_kernel,
+        out_shape=[jax.ShapeDtypeStruct(shape, F32) for shape in shapes],
+        in_specs=[pl.BlockSpec(memory_space=pltpu.SMEM)] + vmem_specs(5),
+        out_specs=vmem_specs(3),
+        compiler_params=pltpu.CompilerParams(vmem_limit_bytes=SMALL_LIMIT),
+        name="pack_parcel",
+    )(where, link_p, link_q, sources, shift, lesser_gain)
+
+
 def vmem_specs(count):
     return [pl.BlockSpec(memory_space=pltpu.VMEM)] * count
 
@@ -333,8 +438,7 @@
     levels, _ = elimination_levels(slabs)
     _, fills = link_places(slabs, mine, levels)
     local = pieces[2].shape[1]
-    shapes = [
-        (groups, energy_groups, mine, per, orb_per, columns),
+    kept = [
         (nodes, width, width),
         (nodes, width, width),
         (nodes, width, width),
@@ -343,18 +447,20 @@
         (fills, width, width),
         (fills, width, width),
         (nodes, width, columns),
-        (nodes, 1, width),
     ]
+    shapes = [(groups, energy_groups, mine, per, orb_per, columns), (nodes, 1, width)] + kept
     return pl.pallas_call(
         functools.partial(retarded_kernel, plan),
         out_shape=[jax.ShapeDtypeStruct(shape, F32) for shape in shapes],
         in_specs=[pl.BlockSpec(memory_space=pltpu.SMEM)] + vmem_specs(len(pieces)),
-        out_specs=vmem_specs(len(shapes)),
-        scratch_shapes=[
+        out_specs=vmem_specs(2) + [pl.BlockSpec(memory_space=pl.ANY)] * len(kept),
+        scratch_shapes=[pltpu.VMEM(shape, F32) for shape in kept]
+        + [
             pltpu.VMEM((slabs, 2 * width + local, columns), F32),
             pltpu.VMEM((nodes, orbits, width), F32),
             pltpu.VMEM((nodes, width, columns), F32),
             pltpu.VMEM((nodes, orbits, width), F32),
+            pltpu.SemaphoreType.DMA((6 * len(levels) + 4,)),
         ],
         compiler_params=pltpu.CompilerParams(vmem_limit_bytes=VMEM_LIMIT),
         name="solve_retarded",
@@ -363,7 +469,7 @@
 
 def solve_lesser(stored, plan):
     (slabs, mine, orbits, groups, energy_groups, per, orb_per) = plan
-    solved = stored[7].shape
+    solved = stored[8].shape
     return pl.pallas_call(
         functools.partial(lesser_kernel, plan),
         out_shape=jax.ShapeDtypeStruct((groups, energy_groups, 2, mine, per, orb_per, solved[-1]), F32),
@@ -430,25 +536,16 @@
     slabs = per * groups
     mine = max(1, local // groups)
     owner = lax.axis_index("slab")
-    factors = jnp.concatenate(
-        [
-            jnp.concatenate([link_p[:, 0], link_p[:, 1]], axis=-1),
-            jnp.concatenate([link_q[:, 0], link_q[:, 1]], axis=-1),
-        ],
-        axis=1,
-    )
     columns_in = sources.reshape(per, width, columns)
-    settings = jnp.swapaxes(jnp.concatenate([shift, lesser_gain], axis=-1), 0, 1)
-    place = lax.axis_index("energy")
-    core = place % 2
-    parcel = jnp.concatenate([jnp.where(core == 0, factors, columns_in), settings], axis=1)
+    core = lax.axis_index("energy") & 1
+    where = jnp.stack([owner * local // groups, owner, core]).astype(jnp.int32)
+    factors, settings, parcel = pack(where, link_p, link_q, sources, shift, lesser_gain)
     siblings = [(j, j ^ 1) for j in range(energy_groups)]
     pieces = [factors, columns_in, settings]
     fetched = [lax.ppermute(parcel, "slab", [(g, g ^ k) for g in range(groups)]) for k in range(1, groups)]
     for piece in fetched:
         pieces.append(piece)
         pieces.append(lax.ppermute(piece, "energy", siblings))
-    where = jnp.stack([owner * local // groups, owner, core]).astype(jnp.int32)
     plan = (slabs, mine, orbits, groups, energy_groups, per, orbits // energy_groups)
     power, *stored = solve_retarded(where, pieces, plan, columns)
 

time: 128 us -> 123 us (0.961)
  Pallas kernels: 51.6 us -> 44.4 us
  local copies, waits for them, and re-layouts: 1.76 us -> 6.16 us
  other arithmetic: 3.2 us -> 0.08 us
  waiting for transfers between devices: 18.1 us -> 19.4 us
    pallas_call x1, Pallas kernels: 30.7 us -> 23.7 us  [solve_retarded(): pl.pallas_call(functools.partial(retarded_kernel, plan), out_shape=[jax.S...]
    unnamed x16 -> x28, local copies, waits for them, and re-layouts: 0.69 us -> 6.16 us
    select_n x1 -> x0, other arithmetic: 1.72 us -> none  [per_device(): jnp.where(core == 0, factors, columns_in)]
  transfers between devices with their start and end apart: 7 -> 7, of which waited for: 6 -> 6; matrix products, arithmetic and copies ran while one was open for 1% -> 0% of each run, Pallas kernels for 11% -> 11%
where the time goes in v4:
time: 123 us
  Pallas kernels  44.4 us (36%)
  blocking collectives  42.2 us (34%)
  waiting for transfers between devices  19.4 us (16%)
  starting transfers between devices  10.3 us (8%)
  local copies, waits for them, and re-layouts  6.16 us (5%)
    all_to_all x1, blocking collectives, spread(): lax.all_to_all(array, ('slab', 'energy'), split_axis=0, concat_axis=0, ti...  42.2 us
    pallas_call x1, Pallas kernels, solve_retarded(): pl.pallas_call(functools.partial(retarded_kernel, plan), out_shape=[jax.S...  23.7 us
    pallas_call x1, Pallas kernels, solve_lesser(): pl.pallas_call(functools.partial(lesser_kernel, plan), out_shape=jax.Shap...  12.9 us
    ppermute x3, waiting for transfers between devices, per_device(): lax.ppermute(parcel, 'slab', [(g, g ^ k) for g in range(groups)])  9.35 us
    all_to_all x1, waiting for transfers between devices, spread(): lax.all_to_all(array, ('slab', 'energy'), split_axis=0, concat_axis=0, ti...  8.8 us
    pallas_call x1, Pallas kernels, correlate(): pl.pallas_call(functools.partial(correlate_kernel, order), grid=(per,), o...  7.08 us
    unnamed x28, local copies, waits for them, and re-layouts  6.16 us
    all_to_all x1, starting transfers between devices, spread(): lax.all_to_all(array, ('slab', 'energy'), split_axis=0, concat_axis=0, ti...  5.57 us
  transfers between devices with their start and end apart: 7, of which 6 were waited for; matrix products, arithmetic and copies ran while one was open for 0% of the time, Pallas kernels for 11%

profile of v4, /device:TPU:0, one launch (start us, length us, event | category | flops | bytes accessed | tf_op | source)
XLA Modules:
  0.0 122.6 jit_solution(11878878543390515727)
XLA Ops:
  0.0 0.7 copy.6.shift_ref
  0.7 0.7 copy.7.gain_ref
  1.4 0.1 pad_add_fusion.where_ref
  1.5 0.9 copy-done
  2.4 0.9 copy-done.2
  3.4 0.9 copy-done.3
  4.3 0.7 pack_parcel.1
  5.0 0.7 copy-done.1
  5.7 0.6 copy-done.4
  6.3 3.9 %collective-permute-start.4 = (f32[3,136,128]{2,1,0:T(8,128)S(1)}, f32[3,136,128]{2,1,0:T(8,128)S(1)}, u32[]{:S(2)}, u32[]{:S(2)}) collective-permute-start(f32[3,136,128]{2,1,0:T(8,128)S(1)} %get-tuple-element.20), channel_id=1, source_target_pairs={{0,24},{8,16},{16,8},{24,0},{1,25},{9,17},{17,9},{25,1},{2,26},{10... | collective-permute-start | bytes 626696 | tf_op jit(solution)/shard_map/ppermute | solution.py:545
  10.2 0.5 collective-permute-start.2
  10.7 0.1 collective-permute-start
  10.7 5.5 %collective-permute-done.4.refs_7_ = f32[3,136,128]{2,1,0:T(8,128)S(1)} collective-permute-done((f32[3,136,128]{2,1,0:T(8,128)S(1)}, f32[3,136,128]{2,1,0:T(8,128)S(1)}, u32[]{:S(2)}, u32[]{:S(2)}) %collective-permute-start.4) | collective-permute-done | bytes 208928 | tf_op jit(solution)/shard_map/ppermute | solution.py:545
  16.2 0.0 collective-permute-start.5
  16.2 3.6 %collective-permute-done.2.refs_5_ = f32[3,136,128]{2,1,0:T(8,128)S(1)} collective-permute-done((f32[3,136,128]{2,1,0:T(8,128)S(1)}, f32[3,136,128]{2,1,0:T(8,128)S(1)}, u32[]{:S(2)}, u32[]{:S(2)}) %collective-permute-start.2) | collective-permute-done | bytes 208928 | tf_op jit(solution)/shard_map/ppermute | solution.py:545
  19.8 0.0 collective-permute-start.3
  19.8 0.3 collective-permute-done.refs_3_
  20.1 0.2 collective-permute-start.1
  20.3 0.0 collective-permute-done.5.refs_8_
  20.3 0.9 collective-permute-done.3.refs_6_
  21.3 0.3 collective-permute-done.1.refs_4_
  21.6 0.0 copy-done.7
  21.6 0.0 copy-done.9
  21.6 0.0 copy-done.10
  21.6 0.4 copy-done.11
  22.0 0.3 copy-done.12
  22.3 23.7 %solve_retarded.1 = (f32[4,8,2,3,8,128]{5,4,3,2,1,0:T(8,128)}, f32[24,1,128]{2,1,0:T(1,128)}, f32[24,128,128]{2,1,0:T(8,128)}, f32[24,128,128]{2,1,0:T(8,128)}, ...) custom-call(s32[3]{0:T(128)} %copy-done.5, ...), custom_call_target="tpu_custom_call" | custom-call | tf_op jit(solution)/shard_map/solve_retarded/pallas_call | solution.py:452
  46.0 5.6 %all-to-all-start = ((f32[32,2,3,8,128]{4,3,2,1,0:T(8,128)}), f32[32,2,3,8,128]{4,3,2,1,0:T(8,128)S(1)}, u32[]{:S(2)}, u32[]{:S(2)}) async-start(f32[32,2,3,8,128]{4,3,2,1,0:T(8,128)} %bitcast.8), calls=%async_computation | async-start | bytes 1572864 | tf_op jit(solution)/shard_map/all_to_all | solution.py:554
  51.6 12.9 %solve_lesser.1 = f32[4,8,2,2,3,8,128]{6,5,4,3,2,1,0:T(8,128)} custom-call(f32[24,1,128]{2,1,0:T(1,128)} %get-tuple-element.22.gains, f32[24,128,128]{2,1,0:T(8,128)} %get-tuple-element.23.inv, f32[24,128,128]{2,1,0:T(8,128)} %get-tuple-element.24.w1, f32[24,128,128]{2,1,0:T(8,128)} %get-tuple-element.25.w2, f32[11,128,128]{2,1,0:T(8,128)} %get-tuple-element.26.up1, ...), custom_call_target="tpu_custom_call" | custom-call | tf_op jit(solution)/shard_map/solve_lesser/pallas_call | solution.py:473
  64.5 8.8 %all-to-all-done.power_ref = f32[32,2,3,8,128]{4,3,2,1,0:T(8,128)S(1)} async-done(((f32[32,2,3,8,128]{4,3,2,1,0:T(8,128)}), f32[32,2,3,8,128]{4,3,2,1,0:T(8,128)S(1)}, u32[]{:S(2)}, u32[]{:S(2)}) %all-to-all-start) | async-done | bytes 786464 | tf_op jit(solution)/shard_map/all_to_all | solution.py:554
  73.3 42.2 %all_to_all.10.got_ref = f32[32,2,2,3,8,128]{5,4,3,2,1,0:T(8,128)} all-to-all(f32[32,2,2,3,8,128]{5,4,3,2,1,0:T(8,128)} %bitcast.7), channel_id=1, replica_groups=mesh['slab'=4,'energy'=8] {'slab','energy'}, dimensions={0} | all-to-all | bytes 3145728 | tf_op jit(solution)/shard_map/all_to_all | solution.py:554
  115.5 7.1 %correlate.1 = f32[2,64,3,8,128]{4,3,2,1,0:T(8,128)} custom-call(f32[32,2,3,8,128]{4,3,2,1,0:T(8,128)} %copy-done.6, f32[32,2,2,3,8,128]{5,4,3,2,1,0:T(8,128)} %all_to_all.10.got_ref), custom_call_target="tpu_custom_call" | custom-call | tf_op jit(solution)/shard_map/correlate/pallas_call | solution.py:515
  (16 shorter events, 0.0 us)
Async XLA Ops:
  1.5 0.9 copy-start
  2.4 0.9 copy-start.2
  3.4 0.9 copy-start.3
  4.3 17.3 %copy-start.5 = (s32[3]{0:T(128)}, s32[3]{0:T(128)S(1)}, u32[]{:S(2)}) copy-start(s32[3]{0:T(128)S(1)} %pad_add_fusion.where_ref) | copy-start | bytes 40
  5.0 0.7 copy-start.1
  5.7 0.6 copy-start.4
  6.3 9.9 %collective-permute-start.4 = (f32[3,136,128]{2,1,0:T(8,128)S(1)}, f32[3,136,128]{2,1,0:T(8,128)S(1)}, u32[]{:S(2)}, u32[]{:S(2)}) collective-permute-start(f32[3,136,128]{2,1,0:T(8,128)S(1)} %get-tuple-element.20), channel_id=1, source_target_pairs={{0,24},{8,16},{16,8},{24,0},{1,25},{9,17},{17,9},{25,1},{2,26},{10... | collective-permute-start | bytes 626696 | tf_op jit(solution)/shard_map/ppermute | solution.py:545
  10.2 9.6 %collective-permute-start.2 = (f32[3,136,128]{2,1,0:T(8,128)S(1)}, f32[3,136,128]{2,1,0:T(8,128)S(1)}, u32[]{:S(2)}, u32[]{:S(2)}) collective-permute-start(f32[3,136,128]{2,1,0:T(8,128)S(1)} %get-tuple-element.20), channel_id=1, source_target_pairs={{0,16},{8,24},{16,0},{24,8},{1,17},{9,25},{17,1},{25,9},{2,18},{10... | collective-permute-start | bytes 626696 | tf_op jit(solution)/shard_map/ppermute | solution.py:545
  10.7 9.4 %collective-permute-start = (f32[3,136,128]{2,1,0:T(8,128)S(1)}, f32[3,136,128]{2,1,0:T(8,128)S(1)}, u32[]{:S(2)}, u32[]{:S(2)}) collective-permute-start(f32[3,136,128]{2,1,0:T(8,128)S(1)} %get-tuple-element.20), channel_id=1, source_target_pairs={{0,8},{8,0},{16,24},{24,16},{1,9},{9,1},{17,25},{25,17},{2,10},{10... | collective-permute-start | bytes 626696 | tf_op jit(solution)/shard_map/ppermute | solution.py:545
  16.2 5.4 %copy-start.7 = (f32[3,136,128]{2,1,0:T(8,128)}, f32[3,136,128]{2,1,0:T(8,128)S(1)}, u32[]{:S(2)}) copy-start(f32[3,136,128]{2,1,0:T(8,128)S(1)} %collective-permute-done.4.refs_7_) | copy-start | bytes 626692
  16.2 4.1 %collective-permute-start.5 = (f32[3,136,128]{2,1,0:T(8,128)S(1)}, f32[3,136,128]{2,1,0:T(8,128)S(1)}, u32[]{:S(2)}, u32[]{:S(2)}) collective-permute-start(f32[3,136,128]{2,1,0:T(8,128)S(1)} %collective-permute-done.4.refs_7_), channel_id=1, source_target_pairs={{0,1},{1,0},{2,3},{3,2},{4,5},{5,4},{6,7},{7,6},{8,9},{9,8},{10,11... | collective-permute-start | bytes 626696 | tf_op jit(solution)/shard_map/ppermute | solution.py:548
  19.8 1.8 %copy-start.8 = (f32[3,136,128]{2,1,0:T(8,128)}, f32[3,136,128]{2,1,0:T(8,128)S(1)}, u32[]{:S(2)}) copy-start(f32[3,136,128]{2,1,0:T(8,128)S(1)} %collective-permute-done.2.refs_5_) | copy-start | bytes 626692
  19.8 1.5 %collective-permute-start.3 = (f32[3,136,128]{2,1,0:T(8,128)S(1)}, f32[3,136,128]{2,1,0:T(8,128)S(1)}, u32[]{:S(2)}, u32[]{:S(2)}) collective-permute-start(f32[3,136,128]{2,1,0:T(8,128)S(1)} %collective-permute-done.2.refs_5_), channel_id=1, source_target_pairs={{0,1},{1,0},{2,3},{3,2},{4,5},{5,4},{6,7},{7,6},{8,9},{9,8},{10,11... | collective-permute-start | bytes 626696 | tf_op jit(solution)/shard_map/ppermute | solution.py:548
  20.1 1.5 %copy-start.9 = (f32[3,136,128]{2,1,0:T(8,128)}, f32[3,136,128]{2,1,0:T(8,128)S(1)}, u32[]{:S(2)}) copy-start(f32[3,136,128]{2,1,0:T(8,128)S(1)} %collective-permute-done.refs_3_) | copy-start | bytes 626692
  20.1 1.5 %collective-permute-start.1 = (f32[3,136,128]{2,1,0:T(8,128)S(1)}, f32[3,136,128]{2,1,0:T(8,128)S(1)}, u32[]{:S(2)}, u32[]{:S(2)}) collective-permute-start(f32[3,136,128]{2,1,0:T(8,128)S(1)} %collective-permute-done.refs_3_), channel_id=1, source_target_pairs={{0,1},{1,0},{2,3},{3,2},{4,5},{5,4},{6,7},{7,6},{8,9},{9,8},{10,11... | collective-permute-start | bytes 626696 | tf_op jit(solution)/shard_map/ppermute | solution.py:548
  20.3 1.3 %copy-start.10 = (f32[3,136,128]{2,1,0:T(8,128)}, f32[3,136,128]{2,1,0:T(8,128)S(1)}, u32[]{:S(2)}) copy-start(f32[3,136,128]{2,1,0:T(8,128)S(1)} %collective-permute-done.5.refs_8_) | copy-start | bytes 626692
  21.3 0.7 copy-start.11
  21.6 0.7 copy-start.12
  46.0 27.3 %all-to-all-start = ((f32[32,2,3,8,128]{4,3,2,1,0:T(8,128)}), f32[32,2,3,8,128]{4,3,2,1,0:T(8,128)S(1)}, u32[]{:S(2)}, u32[]{:S(2)}) async-start(f32[32,2,3,8,128]{4,3,2,1,0:T(8,128)} %bitcast.8), calls=%async_computation | async-start | bytes 1572864 | tf_op jit(solution)/shard_map/all_to_all | solution.py:554
  73.3 42.2 %copy-start.6 = (f32[32,2,3,8,128]{4,3,2,1,0:T(8,128)}, f32[32,2,3,8,128]{4,3,2,1,0:T(8,128)S(1)}, u32[]{:S(2)}) copy-start(f32[32,2,3,8,128]{4,3,2,1,0:T(8,128)S(1)} %all-to-all-done.power_ref) | copy-start | bytes 2359300
